TPU v7x, 256 devices: a whole 4x4x8 slice. The times are simulated.
256 devices in a mesh: attn: 16 (over x, y), exp: 8 (over z), mb: 2 (over core).
Axes of the slice: x: 4, y: 4, z: 8, core: 2. Of those that a mesh axis runs over, the one named last changes fastest.
Arguments:
- resid: bfloat16 [2048, 6144], P(('attn', 'mb')), may hold values from -6 to 6
- norm_gain: bfloat16 [6144], replicated, may hold values from 0.099609375 to 1.8984375
- router: bfloat16 [6144, 8], replicated, may hold values from -0.078125 to 0.078125
- expert_ids: int32 [2048, 2], P(('attn', 'mb')), may hold values from 0 to 7, all different within a row; in each aligned block of 64 rows (0 to 63, 64 to 127, ...) at most 24 rows name the same one
- w_gate: bfloat16 [8, 6144, 8192], P('exp', None, ('attn', 'mb')), may hold values from -0.078125 to 0.078125
- w_up: bfloat16 [8, 6144, 8192], P('exp', None, ('attn', 'mb')), may hold values from -0.078125 to 0.078125
- w_down: bfloat16 [8, 8192, 6144], P('exp', ('attn', 'mb')), may hold values from -0.0625 to 0.0625
Outputs:
- mixed: bfloat16 [2048, 6144], P(('attn', 'mb'))
Inputs may be any that keep to these rules, and one draw needn't show every extreme that they name: `expert_ids`: the two experts of a row differ. Among the rows of one device no expert is chosen by more than 24 rows, and some expert is chosen by exactly 24 of them.
All inputs are finite; a program needn't handle non-finite values.
Results may differ from a plain program's by a relative error of at most 0.012.
Values may be sent and summed in bfloat16 or wider, within the bound.
A program may use at most 128 MiB of HBM per device.

v0:
```python
import jax
import jax.numpy as jnp
from jax import lax
from jax.sharding import PartitionSpec as P

EXPERTS = 8
CAP = 24


def slot_table(chosen_ids, experts, capacity):
    rows = chosen_ids.shape[-2]
    flat = chosen_ids.reshape(chosen_ids.shape[:-2] + (rows * 2,))
    onehot = (flat[..., None] == jnp.arange(experts, dtype=jnp.int32)).astype(jnp.int32)
    before = jnp.cumsum(onehot, axis=-2) - onehot
    position = jnp.sum(before * onehot, axis=-1)
    target = flat * capacity + position
    return (target[..., None] == jnp.arange(experts * capacity, dtype=jnp.int32)).astype(
        jnp.bfloat16
    )


def apply_experts(blocks, w_gate, w_up, w_down):
    gate = jnp.einsum("gjcd,jdf->gjcf", blocks, w_gate, preferred_element_type=jnp.float32)
    upper = jnp.einsum("gjcd,jdf->gjcf", blocks, w_up, preferred_element_type=jnp.float32)
    hidden = (jax.nn.silu(gate) * upper).astype(jnp.bfloat16)
    return jnp.einsum("gjcf,jfd->gjcd", hidden, w_down, preferred_element_type=jnp.float32)


def per_device(resid, norm_gain, router, expert_ids, w_gate, w_up, w_down):
    rows = resid.shape[0]
    width = resid.shape[1]
    local = w_gate.shape[0]
    groups = lax.axis_size(("attn", "mb"))
    floats = resid.astype(jnp.float32)
    scale = lax.rsqrt(jnp.mean(floats * floats, axis=-1, keepdims=True) + 1e-05)
    normed = (floats * scale * norm_gain.astype(jnp.float32)).astype(jnp.bfloat16)
    logits = jnp.dot(normed, router, preferred_element_type=jnp.float32)
    chosen = jnp.take_along_axis(logits, expert_ids, axis=1)
    first = jax.nn.sigmoid(chosen[:, 0] - chosen[:, 1])
    second = jax.nn.sigmoid(chosen[:, 1] - chosen[:, 0])
    pair_weights = jnp.stack([first, second], axis=1)
    table = slot_table(expert_ids, EXPERTS, CAP)
    offset = lax.axis_index("exp") * (local * CAP)
    local_table = lax.dynamic_slice_in_dim(table, offset, local * CAP, 1)
    pairs = jnp.repeat(normed, 2, axis=0)
    outgoing = jnp.einsum(
        "as,ad->sd", local_table, pairs, preferred_element_type=jnp.float32
    ).astype(jnp.bfloat16)
    grouped = lax.all_gather(outgoing, ("attn", "mb"), axis=0, tiled=True)
    blocks = grouped.reshape(groups, local, CAP, width)
    partial_value = apply_experts(blocks, w_gate, w_up, w_down).reshape(groups, local * CAP, width)
    summed = lax.psum_scatter(
        partial_value.astype(jnp.bfloat16), ("attn", "mb"), scatter_dimension=0, tiled=True
    ).astype(jnp.float32)
    finished = summed.reshape(local * CAP, width).astype(jnp.bfloat16)
    every_out = lax.all_gather(finished, "exp", axis=0, tiled=True)
    picked = jnp.einsum("as,sd->ad", table, every_out, preferred_element_type=jnp.float32).reshape(
        rows, 2, width
    )
    total = jnp.sum(pair_weights[:, :, None] * picked, axis=1)
    return (floats + total).astype(jnp.bfloat16)


def solution(mesh):
    in_specs = (
        P(("attn", "mb"), None),
        P(),
        P(),
        P(("attn", "mb"), None),
        P("exp", None, ("attn", "mb")),
        P("exp", None, ("attn", "mb")),
        P("exp", ("attn", "mb"), None),
    )
    out_specs = P(("attn", "mb"), None)
    return jax.shard_map(
        per_device, mesh=mesh, in_specs=in_specs, out_specs=out_specs, check_vma=False
    )
```

profile of v0, /device:TPU:2, one launch (start us, length us, event | category | flops | bytes accessed | tf_op | source)
XLA Modules:
  0.0 282.5 jit_solution(18330568596634457349)
XLA Ops:
  6.5 0.0 copy-start
  6.5 0.0 all-gather.4.cloned.1.call-start
  6.5 1.5 fusion.7
  8.1 0.7 convert_element_type.31
  8.8 0.8 copy.46
  9.6 0.1 reshape.63
  9.7 0.1 fusion.34
  9.8 0.2 reduce_window_sum.11
  10.0 0.2 select_reduce_fusion
  10.2 0.1 iota_compare_fusion
  10.3 1.4 fusion.9
  11.7 0.0 copy-start.1
  11.7 0.9 copy-done.1
  12.6 2.1 broadcast_in_dim.7
  14.7 4.5 %reshape.64 = bf16[128,6144]{1,0:T(8,128)(2,1)} reshape(bf16[64,2,6144]{2,1,0:T(2,128)(2,1)} %broadcast_in_dim.7) | data formatting | bytes 3145728 | tf_op jit(solution)/shard_map/reshape | solution.py:45
  19.2 2.6 convolution_convert_fusion.1
  21.8 0.0 all-gather.4.cloned.1.call-update
  21.8 0.0 reduce-scatter.2.cloned.1.call-start
  21.9 63.5 %all-gather.4.cloned.1.call-done = bf16[768,6144]{1,0:T(8,128)(2,1)} async-done(((bf16[24,6144]{1,0:T(8,128)(2,1)}), bf16[768,6144]{1,0:T(8,128)(2,1)}) %all-gather.4.cloned.1.call-update) | async-done | bytes 9437200 | tf_op jit(solution)/shard_map/all_gather | solution.py:49
  85.4 8.1 %fusion.11 = f32[32,1,24,256]{3,2,0,1:T(8,128)} fusion(bf16[32,24,6144]{2,1,0:T(8,128)(2,1)} %bitcast.61, bf16[1,6144,256]{2,1,0:T(8,128)(2,1)} %param.11), kind=kOutput, calls=%fused_computation.18 | convolution fusion | flops 2415919104 | bytes 13369344 | tf_op jit(solution)/shard_map/gjcd,jdf->gjcf/dot_general | solution.py:23
  93.4 0.0 copy-done
  93.4 20.0 %convolution_convert_fusion = bf16[32,24,6144]{2,1,0:T(8,128)(2,1)} fusion(bf16[1,256,6144]{2,1,0:T(8,128)(2,1)S(1)} %copy-done, bf16[32,24,6144]{2,1,0:T(8,128)(2,1)} %bitcast.62, bf16[1,6144,256]{2,1,0:T(8,128)(2,1)} %param.12, f32[32,1,24,256]{3,2,0,1:T(8,128)} %fusion.11), kind=kOutput, calls=%fused_computation.1 | convolution fusion | flops 4837736448 | bytes 25952256 | tf_op jit(solution)/shard_map/gjcf,jfd->gjcd/dot_general | solution.py:26
  113.5 0.0 copy-start.4
  113.5 0.0 copy-start.3
  113.5 0.0 reduce-scatter.2.cloned.1.call-update
  113.5 0.2 all-gather.6.cloned.1.call-start
  113.7 102.4 %reduce-scatter.2.cloned.1.call-done = bf16[1,24,6144]{2,1,0:T(8,128)(2,1)} async-done(((bf16[32,24,6144]{2,1,0:T(8,128)(2,1)}), bf16[1,24,6144]{2,1,0:T(8,128)(2,1)}) %reduce-scatter.2.cloned.1.call-update) | async-done | bytes 294928 | tf_op jit(solution)/shard_map/reduce_scatter | solution.py:52
  216.1 0.0 all-gather.6.cloned.1.call-update
  216.1 0.0 copy-done.4
  216.2 0.1 copy.43
  216.3 0.1 reshape.71
  216.4 0.0 copy-done.3
  216.4 1.4 fusion.38
  217.8 1.0 gather_fusion
  218.9 0.1 reshape.74
  219.0 0.1 copy.44
  219.1 0.1 copy.45
  219.2 40.1 %all-gather.6.cloned.1.call-done = bf16[1,192,6144]{2,1,0:T(8,128)(2,1)} async-done(((bf16[1,24,6144]{2,1,0:T(8,128)(2,1)}), bf16[1,192,6144]{2,1,0:T(8,128)(2,1)}) %all-gather.6.cloned.1.call-update) | async-done | bytes 2359312 | tf_op jit(solution)/shard_map/all_gather | solution.py:56
  259.3 3.9 %fusion.5 = f32[128,6144]{1,0:T(8,128)} fusion(bf16[1,192,6144]{2,1,0:T(8,128)(2,1)} %all-gather.6.cloned.1.call-done, s32[128]{0:T(128)S(1)} %multiply_add_fusion), kind=kOutput, calls=%fused_computation.12 | convolution fusion | flops 302014464 | bytes 5505536 | tf_op jit(solution)/shard_map/as,sd->ad/dot_general | solution.py:57
  263.3 5.0 %reshape.70 = f32[64,2,6144]{2,1,0:T(2,128)} reshape(f32[128,6144]{1,0:T(8,128)} %fusion.5) | data formatting | bytes 6291456 | tf_op jit(solution)/shard_map/reshape | solution.py:57
  268.2 0.0 copy-start.2
  268.3 6.7 %multiply_reduce_fusion = f32[64,6144]{1,0:T(8,128)S(1)} fusion(f32[64,2,6144]{2,1,0:T(2,128)} %reshape.70, f32[64,2]{1,0:T(8,128)S(1)} %copy.45), kind=kLoop, calls=%fused_computation.8 | loop fusion | flops 1179648 | bytes 4719104 | tf_op jit(solution)/shard_map/reduce_sum | solution.py:60
  274.9 0.0 copy-done.2
  274.9 1.0 fusion.10
  (6 shorter events, 0.1 us)
Async XLA Ops:
  6.5 86.9 %copy-start = (bf16[1,256,6144]{2,1,0:T(8,128)(2,1)S(1)}, bf16[1,256,6144]{2,1,0:T(8,128)(2,1)}, u32[]{:S(2)}) copy-start(bf16[1,256,6144]{2,1,0:T(8,128)(2,1)} %param.13) | copy-start | bytes 9437188
  6.5 78.8 %all-gather.4.cloned.1.call-start = ((), (), s32[]{:S(2)}) async-start(), calls=%async_computation.1 | async-start | bytes 9732096 | tf_op jit(solution)/shard_map/all_gather | solution.py:49
  11.7 0.9 copy-start.1
  21.8 194.3 %reduce-scatter.2.cloned.1.call-start = ((), (), s32[]{:S(2)}) async-start(), calls=%async_computation.2 | async-start | bytes 9732096 | tf_op jit(solution)/shard_map/reduce_scatter | solution.py:52
  113.5 102.7 %copy-start.4 = (s32[64,2]{0,1:T(2,128)S(1)}, s32[64,2]{0,1:T(2,128)}, u32[]{:S(2)}) copy-start(s32[64,2]{0,1:T(2,128)} %param.10) | copy-start | bytes 1540
  113.5 102.9 %copy-start.3 = (bf16[6144,8]{0,1:T(8,128)(2,1)S(1)}, bf16[6144,8]{0,1:T(8,128)(2,1)}, u32[]{:S(2)}) copy-start(bf16[6144,8]{0,1:T(8,128)(2,1)} %param.9) | copy-start | bytes 294916
  113.5 145.8 %all-gather.6.cloned.1.call-start = ((), (), s32[]{:S(2)}) async-start(), calls=%async_computation.3 | async-start | bytes 2654208 | tf_op jit(solution)/shard_map/all_gather | solution.py:56
  268.2 6.7 %copy-start.2 = (bf16[64,6144]{1,0:T(8,128)(2,1)S(1)}, bf16[64,6144]{1,0:T(8,128)(2,1)}, u32[]{:S(2)}) copy-start(bf16[64,6144]{1,0:T(8,128)(2,1)} %param.7) | copy-start | bytes 2359300
Sparse Core Ops, SparseCore 0:
  21.9 63.3 all-gather.3
  113.6 102.4 reduce-scatter.1
  218.0 41.2 all-gather.5
where the time goes:
time: 283 us; the launch traced here: 282 us
  waiting for transfers between devices  206 us (73%)
  matrix products  36.1 us (13%)
  local copies, waits for them, and re-layouts  15 us (5%)
  between operations  13.2 us (5%)
  other arithmetic  11.9 us (4%)
    reduce_scatter x1, waiting for transfers between devices, per_device(): lax.psum_scatter(partial_value.astype(jnp.bfloat16), ('attn', 'mb'), scat...  102 us
    all_gather x1, waiting for transfers between devices, per_device(): grouped = lax.all_gather(outgoing, ('attn', 'mb'), axis=0, tiled=True)  63.5 us
    all_gather x1, waiting for transfers between devices, per_device(): every_out = lax.all_gather(finished, 'exp', axis=0, tiled=True)  40.1 us
    dot_general x1, matrix products, apply_experts(): jnp.einsum('gjcf,jfd->gjcd', hidden, w_down, preferred_element_type=jnp.f...  20 us
    dot_general x1, matrix products, apply_experts(): jnp.einsum('gjcd,jdf->gjcf', blocks, w_gate, preferred_element_type=jnp.f...  8.05 us
    reduce_sum x1, other arithmetic, per_device(): total = jnp.sum(pair_weights[:, :, None] * picked, axis=1)  6.66 us
  transfers between devices with their start and end apart: 3, of which 3 were waited for; matrix products, arithmetic and copies ran while one was open for 1% of the time, Pallas kernels for 0%

commit v1 on v0

v1 whole, which is shorter than its diff:
```python
import jax
import jax.numpy as jnp
from jax import lax
from jax.experimental import pallas as pl
from jax.experimental.pallas import tpu as pltpu
from jax.sharding import PartitionSpec as P

EXPERTS = 8
CAP = 24
ROWS = 64
D = 6144
HALF = D // 2
F = 256
SIDE = 4
LAYERS = 8
CHUNKS = 6
CW = D // CHUNKS
HW = CW // 2
OW = CW // LAYERS
STAGES = 7
MESH = pl.DeviceIdType.MESH
BF = jnp.bfloat16
F32 = jnp.float32


def dot(a, b):
    return jnp.dot(a, b, preferred_element_type=F32)


def kernel(
    resid_h, gain, router_t, ids, ids_t, wg_h, wu_h, wd_h, out_h,
    res, rows, wg, wu, wd, hid,
    p0, p1, p3, t1, t2, t3, qh, qf,
    v0, v1, v3, s1, s2, s3, ph, pf,
    eo, ec, table, om,
    load_sem, sib_send, sib_recv, a_send, a_recv,
    qh_send, qh_recv, qf_send, qf_recv, ph_send, ph_recv, pf_send, pf_recv,
    e_send, e_recv, o_send, o_recv, out_sem,
):
    attn, z, c = lax.axis_index("attn"), lax.axis_index("exp"), lax.axis_index("mb")
    x, y = attn // SIDE, attn % SIDE

    def plane(dx, dy):
        return {"attn": ((x + dx) % SIDE) * SIDE + (y + dy) % SIDE, "exp": z, "mb": c}

    def on_p(d):
        d = d % SIDE
        return plane((1 - c) * d, c * d)

    def on_q(d):
        d = d % SIDE
        return plane(c * d, (1 - c) * d)

    def on_z(d):
        return {"attn": attn, "exp": (z + d) % LAYERS, "mb": c}

    sibling = {"attn": attn, "exp": z, "mb": 1 - c}

    load_res = pltpu.make_async_copy(resid_h, res, load_sem.at[0])
    load_res.start()
    loads = [
        pltpu.make_async_copy(src.at[0], dst.at[0], load_sem.at[1 + i])
        for i, (src, dst) in enumerate(((wg_h, wg), (wu_h, wu), (wd_h, wd)))
    ]

    barrier = pltpu.get_barrier_semaphore()
    partners = [on_p(1), on_p(-1), on_q(1), on_q(-1), sibling] + [on_z(d) for d in range(1, LAYERS)]
    for device in partners:
        pl.semaphore_signal(barrier, inc=1, device_id=device, device_id_type=MESH)
    for load in loads:
        load.start()

    hit = ((ids_t[0:1, :] == z) | (ids_t[1:2, :] == z)).astype(F32)
    hits = jnp.broadcast_to(hit, (8, ROWS)).astype(BF)
    upper = (
        lax.broadcasted_iota(jnp.int32, (ROWS, ROWS), 0)
        < lax.broadcasted_iota(jnp.int32, (ROWS, ROWS), 1)
    ).astype(F32).astype(BF)
    rank = dot(hits, upper)[0:1, :]
    slot = lax.broadcasted_iota(jnp.int32, (CAP, ROWS), 0).astype(F32)
    pick = jnp.where((rank == slot) & (hit > 0.5), 1.0, 0.0).astype(BF)

    load_res.wait()
    square = jnp.zeros((CAP, CW), F32)
    for k in range(CHUNKS):
        cols = pl.ds(k * CW, CW)
        part = dot(pick, res[:, cols])
        t1_part = part.astype(BF)
        rows[0, 0, :, cols] = t1_part
        square = square + part * part
    scale = lax.rsqrt(jnp.sum(square, axis=1, keepdims=True) / D + 1e-05)
    for k in range(CHUNKS):
        cols = pl.ds(k * CW, CW)
        part = rows[0, 0, :, cols].astype(F32)
        rows[0, 0, :, cols] = (part * scale * gain[:, cols].astype(F32)).astype(BF)

    pl.semaphore_wait(barrier, len(partners))

    def remote(src, dst, send, recv, device):
        return pltpu.make_async_remote_copy(
            src_ref=src, dst_ref=dst, send_sem=send, recv_sem=recv,
            device_id=device, device_id_type=MESH,
        )

    sent = []

    def a_copy(pr, qr, to_pr, to_qr, half, device):
        n = len(sent)
        src, dst = rows.at[pr, qr], rows.at[to_pr, to_qr]
        if half is not None:
            part = pl.ds(half * HALF, HALF)
            src, dst = src.at[:, part], dst.at[:, part]
        copy = remote(src, dst, a_send.at[n], a_recv.at[to_pr, to_qr, half or 0], device)
        copy.start()
        sent.append(copy)

    def a_wait(pr, qr, halves=False):
        for half in range(2 if halves else 1):
            ref = rows.at[pr, qr]
            if halves:
                ref = ref.at[:, pl.ds(half * HALF, HALF)]
            remote(ref, ref, a_send.at[0], a_recv.at[pr, qr, half], sibling).wait_recv()

    a_copy(0, 0, 3, 0, None, on_p(1))
    a_copy(0, 0, 1, 0, None, on_p(-1))
    a_copy(0, 0, 0, 3, None, on_q(1))
    a_copy(0, 0, 0, 1, None, on_q(-1))

    siblings = []
    for i, (src, dst) in enumerate(((wg_h, wg), (wu_h, wu), (wd_h, wd))):
        copy = remote(src.at[0], dst.at[1], sib_send.at[i], sib_recv.at[i], sibling)
        copy.start()
        siblings.append(copy)

    square = jnp.zeros((ROWS, CW), F32)
    for k in range(CHUNKS):
        part = res[:, pl.ds(k * CW, CW)].astype(F32)
        square = square + part * part
    scale = lax.rsqrt(jnp.sum(square, axis=1, keepdims=True) / D + 1e-05)
    logits = jnp.zeros((ROWS, EXPERTS), F32)
    for k in range(CHUNKS):
        cols = pl.ds(k * CW, CW)
        normed = (res[:, cols].astype(F32) * scale * gain[:, cols].astype(F32)).astype(BF)
        logits = logits + lax.dot_general(
            normed, router_t[:, cols], (((1,), (1,)), ((), ())), preferred_element_type=F32
        )
    expert = lax.broadcasted_iota(jnp.int32, (ROWS, EXPERTS), 1)
    id_a, id_b = ids[:, 0:1], ids[:, 1:2]
    of_a = jnp.sum(jnp.where(expert == id_a, logits, 0.0), axis=1, keepdims=True)
    of_b = jnp.sum(jnp.where(expert == id_b, logits, 0.0), axis=1, keepdims=True)
    first, second = jax.nn.sigmoid(of_a - of_b), jax.nn.sigmoid(of_b - of_a)
    near = (expert + z) % EXPERTS
    chose_a, chose_b = near == id_a, near == id_b
    chosen = jnp.where(chose_a | chose_b, 1.0, 0.0)
    weight = jnp.where(chose_a, first, 0.0) + jnp.where(chose_b, second, 0.0)
    weight_hi = weight.astype(BF)
    weight_lo = (weight - weight_hi.astype(F32)).astype(BF)
    lower = (
        lax.broadcasted_iota(jnp.int32, (ROWS, ROWS), 0)
        > lax.broadcasted_iota(jnp.int32, (ROWS, ROWS), 1)
    ).astype(F32).astype(BF)
    ranks = dot(lower, chosen.astype(BF))
    wide = EXPERTS * CAP
    start = lax.broadcasted_iota(jnp.int32, (EXPERTS, wide), 0) * CAP
    lane = lax.broadcasted_iota(jnp.int32, (EXPERTS, wide), 1)
    spread = jnp.where((lane >= start) & (lane < start + CAP), 1.0, 0.0).astype(BF)
    place = (lax.broadcasted_iota(jnp.int32, (ROWS, wide), 1) % CAP).astype(F32)
    here = (dot(ranks.astype(BF), spread) == place) & (dot(chosen.astype(BF), spread) > 0.5)
    table[0:ROWS, :] = jnp.where(here, dot(weight_hi, spread), 0.0).astype(BF)
    table[ROWS:, :] = jnp.where(here, dot(weight_lo, spread), 0.0).astype(BF)

    def hidden(pr, s):
        lhs = rows[pr].reshape(SIDE * CAP, D)
        gate = dot(lhs, wg[s])
        upper_value = dot(lhs, wu[s])
        value = gate / (1.0 + jnp.exp(-gate)) * upper_value
        hid[pl.ds(pr * SIDE * CAP, SIDE * CAP), pl.ds(s * F, F)] = value.astype(BF)

    def forward_q(pr):
        a_wait(pr, 1)
        a_copy(pr, 1, pr, 2, 0, on_q(-1))
        a_wait(pr, 3)
        a_copy(pr, 3, pr, 2, 1, on_q(1))

    def spread_q(pr):
        a_copy(pr, 0, pr, 3, None, on_q(1))
        a_copy(pr, 0, pr, 1, None, on_q(-1))

    a_wait(1, 0)
    a_copy(1, 0, 2, 0, 0, on_p(-1))
    a_wait(3, 0)
    a_copy(3, 0, 2, 0, 1, on_p(1))
    forward_q(0)
    spread_q(1)
    spread_q(3)
    a_wait(2, 0, True)
    spread_q(2)
    a_wait(0, 2, True)
    loads[0].wait()
    loads[1].wait()
    hidden(0, 0)
    forward_q(1)
    siblings[0].wait_recv()
    siblings[1].wait_recv()
    hidden(0, 1)
    forward_q(3)
    a_wait(1, 2, True)
    hidden(1, 0)
    hidden(1, 1)
    forward_q(2)
    a_wait(3, 2, True)
    hidden(3, 0)
    hidden(3, 1)
    a_wait(2, 2, True)
    hidden(2, 0)
    hidden(2, 1)
    loads[2].wait()
    siblings[2].wait_recv()

    def ds_full(k):
        return pl.ds(pl.multiple_of(k * CW, CW), CW)

    def ds_half(k, half):
        return pl.ds(pl.multiple_of(k * CW + half * HW, HW), HW)

    def ds_pack(k):
        return pl.ds(pl.multiple_of(k * HW, HW), HW)

    def ds_own(k):
        return pl.ds(pl.multiple_of(k * OW, OW), OW)

    def ds_layer(k, layer):
        return pl.ds(pl.multiple_of(k * CW + layer * OW, OW), OW)

    def q_half(k, side):
        return remote(
            t2.at[:, :, ds_half(k, side)], qh.at[side, :, :, ds_pack(k)],
            qh_send.at[k, side], qh_recv.at[k, side], on_q(1 - 2 * side),
        )

    def q_full(k, side):
        return remote(
            (t1, t3)[side].at[:, :, ds_full(k)], qf.at[side, :, :, ds_full(k)],
            qf_send.at[k, side], qf_recv.at[k, side], on_q(1 - 2 * side),
        )

    def p_half(k, side):
        return remote(
            s2.at[:, ds_half(k, side)], ph.at[side, :, ds_pack(k)],
            ph_send.at[k, side], ph_recv.at[k, side], on_p(1 - 2 * side),
        )

    def p_full(k, side):
        return remote(
            (s1, s3)[side].at[:, ds_full(k)], pf.at[side, :, ds_full(k)],
            pf_send.at[k, side], pf_recv.at[k, side], on_p(1 - 2 * side),
        )

    def e_copy(k, d):
        return remote(
            eo.at[:, ds_layer(k, (z + d) % LAYERS)], ec.at[LAYERS - d, :, ds_own(k)],
            e_send.at[k, d - 1], e_recv.at[k, LAYERS - d - 1], on_z(d),
        )

    def e_arrived(k, d):
        return remote(
            eo.at[:, ds_layer(k, (z + d) % LAYERS)], ec.at[d, :, ds_own(k)],
            e_send.at[k, d - 1], e_recv.at[k, d - 1], on_z(d),
        )

    def o_copy(k, d):
        return remote(
            om.at[:, ds_layer(k, z)], om.at[:, ds_layer(k, z)],
            o_send.at[k, d - 1], o_recv.at[k, LAYERS - d - 1], on_z(d),
        )

    def o_arrived(k, d):
        there = om.at[:, ds_layer(k, (z + d) % LAYERS)]
        return remote(there, there, o_send.at[k, d - 1], o_recv.at[k, d - 1], on_z(d))

    def out_copy(k):
        return pltpu.make_async_copy(om.at[:, ds_full(k)], out_h.at[:, ds_full(k)], out_sem.at[k])

    def stage_down(k):
        cols = ds_full(k)
        value = dot(hid[:, 0:F], wd[0, :, cols]) + dot(hid[:, F:], wd[1, :, cols])
        value = value.reshape(SIDE, SIDE, CAP, CW)
        t2[:, :, cols] = value[:, 2].astype(BF)
        q_half(k, 0).start()
        q_half(k, 1).start()
        p0[:, :, cols] = value[:, 0]
        p1[:, :, cols] = value[:, 1]
        p3[:, :, cols] = value[:, 3]

    def stage_q_half(k):
        low, high, pack = ds_half(k, 0), ds_half(k, 1), ds_pack(k)
        q_half(k, 0).wait_recv()
        t1[:, :, low] = (p1[:, :, low] + qh[0, :, :, pack].astype(F32)).astype(BF)
        t1[:, :, high] = p1[:, :, high].astype(BF)
        q_full(k, 0).start()
        q_half(k, 1).wait_recv()
        t3[:, :, low] = p3[:, :, low].astype(BF)
        t3[:, :, high] = (p3[:, :, high] + qh[1, :, :, pack].astype(F32)).astype(BF)
        q_full(k, 1).start()

    def stage_q_full(k):
        cols = ds_full(k)
        q_full(k, 0).wait_recv()
        q_full(k, 1).wait_recv()

        def summed(pr):
            return p0[pr, :, cols] + qf[0, pr, :, cols].astype(F32) + qf[1, pr, :, cols].astype(F32)

        s2[:, cols] = summed(2).astype(BF)
        p_half(k, 0).start()
        p_half(k, 1).start()
        v1[:, cols] = summed(1)
        v3[:, cols] = summed(3)
        v0[:, cols] = summed(0)

    def stage_p_half(k):
        low, high, pack = ds_half(k, 0), ds_half(k, 1), ds_pack(k)
        p_half(k, 0).wait_recv()
        s1[:, low] = (v1[:, low] + ph[0, :, pack].astype(F32)).astype(BF)
        s1[:, high] = v1[:, high].astype(BF)
        p_full(k, 0).start()
        p_half(k, 1).wait_recv()
        s3[:, low] = v3[:, low].astype(BF)
        s3[:, high] = (v3[:, high] + ph[1, :, pack].astype(F32)).astype(BF)
        p_full(k, 1).start()

    def stage_p_full(k):
        cols = ds_full(k)
        p_full(k, 0).wait_recv()
        p_full(k, 1).wait_recv()
        total = v0[:, cols] + pf[0, :, cols].astype(F32) + pf[1, :, cols].astype(F32)
        eo[:, cols] = total.astype(BF)
        for d in range(1, LAYERS):
            e_copy(k, d).start()

    def stage_mix(k):
        mine = ds_layer(k, z)
        for d in range(1, LAYERS):
            e_arrived(k, d).wait_recv()
        ec[0, :, ds_own(k)] = eo[:, mine]
        every = ec[:, :, ds_own(k)].astype(F32).reshape(LAYERS * CAP, OW).astype(BF)
        both = dot(table[...], every)
        om[:, mine] = (res[:, mine].astype(F32) + (both[:ROWS] + both[ROWS:])).astype(BF)
        for d in range(1, LAYERS):
            o_copy(k, d).start()

    def stage_out(k):
        for d in range(1, LAYERS):
            o_arrived(k, d).wait_recv()
        out_copy(k).start()

    stages = [stage_down, stage_q_half, stage_q_full, stage_p_half, stage_p_full, stage_mix, stage_out]

    def step(i, carry):
        for s, stage in enumerate(stages):
            @pl.when((i >= s) & (i < s + CHUNKS))
            def _(s=s, stage=stage):
                stage(i - s)
        return carry

    lax.fori_loop(0, CHUNKS + STAGES - 1, step, 0)

    for copy in sent:
        copy.wait_send()
    for copy in siblings:
        copy.wait_send()

    def finish(k, carry):
        for side in range(2):
            q_half(k, side).wait_send()
            q_full(k, side).wait_send()
            p_half(k, side).wait_send()
            p_full(k, side).wait_send()
        for d in range(1, LAYERS):
            e_copy(k, d).wait_send()
            o_copy(k, d).wait_send()
        out_copy(k).wait()
        return carry

    lax.fori_loop(0, CHUNKS, finish, 0)


def per_device(resid, norm_gain, router, expert_ids, w_gate, w_up, w_down):
    vmem, hbm = pl.BlockSpec(memory_space=pltpu.VMEM), pl.BlockSpec(memory_space=pl.ANY)
    dma = pltpu.SemaphoreType.DMA
    block = (SIDE, CAP, D)
    return pl.pallas_call(
        kernel,
        name="expert_block",
        out_shape=jax.ShapeDtypeStruct((ROWS, D), BF),
        in_specs=[hbm, vmem, vmem, vmem, vmem, hbm, hbm, hbm],
        out_specs=hbm,
        scratch_shapes=[
            pltpu.VMEM((ROWS, D), BF),
            pltpu.VMEM((SIDE, SIDE, CAP, D), BF),
            pltpu.VMEM((2, D, F), BF),
            pltpu.VMEM((2, D, F), BF),
            pltpu.VMEM((2, F, D), BF),
            pltpu.VMEM((SIDE * SIDE * CAP, 2 * F), BF),
            pltpu.VMEM(block, F32),
            pltpu.VMEM(block, F32),
            pltpu.VMEM(block, F32),
            pltpu.VMEM(block, BF),
            pltpu.VMEM(block, BF),
            pltpu.VMEM(block, BF),
            pltpu.VMEM((2, SIDE, CAP, HALF), BF),
            pltpu.VMEM((2, SIDE, CAP, D), BF),
            pltpu.VMEM((CAP, D), F32),
            pltpu.VMEM((CAP, D), F32),
            pltpu.VMEM((CAP, D), F32),
            pltpu.VMEM((CAP, D), BF),
            pltpu.VMEM((CAP, D), BF),
            pltpu.VMEM((CAP, D), BF),
            pltpu.VMEM((2, CAP, HALF), BF),
            pltpu.VMEM((2, CAP, D), BF),
            pltpu.VMEM((CAP, D), BF),
            pltpu.VMEM((LAYERS, CAP, D // LAYERS), BF),
            pltpu.VMEM((2 * ROWS, EXPERTS * CAP), BF),
            pltpu.VMEM((ROWS, D), BF),
            dma((4,)),
            dma((3,)),
            dma((3,)),
            dma((20,)),
            dma((SIDE, SIDE, 2)),
        ]
        + [dma((CHUNKS, 2))] * 8
        + [dma((CHUNKS, LAYERS - 1))] * 4
        + [dma((CHUNKS,))],
        compiler_params=pltpu.CompilerParams(
            collective_id=0, has_side_effects=True, vmem_limit_bytes=60 * 1024 * 1024
        ),
    )(
        resid, norm_gain.reshape(1, D), router.T, expert_ids, expert_ids.T, w_gate, w_up, w_down
    )


def solution(mesh):
    in_specs = (
        P(("attn", "mb"), None),
        P(),
        P(),
        P(("attn", "mb"), None),
        P("exp", None, ("attn", "mb")),
        P("exp", None, ("attn", "mb")),
        P("exp", ("attn", "mb"), None),
    )
    out_specs = P(("attn", "mb"), None)
    return jax.shard_map(
        per_device, mesh=mesh, in_specs=in_specs, out_specs=out_specs, check_vma=False
    )
```

time: 283 us -> 100 us (0.35)
  waiting for transfers between devices: 206 us -> 0 us
  Pallas kernels: 0 us -> 95 us
  matrix products: 36.1 us -> 0 us
  between operations: 13.2 us -> 0.01 us
  other arithmetic: 11.9 us -> 0 us
  local copies, waits for them, and re-layouts: 15 us -> 4.76 us
    all_gather x2 -> x0, waiting for transfers between devices: 104 us -> none  [the longest x1 63.5 us: per_device(): grouped = lax.all_gather(outgoing, ('attn', 'mb'), axis=0, tiled=True)]
    reduce_scatter x1 -> x0, waiting for transfers between devices: 102 us -> none  [per_device(): lax.psum_scatter(partial_value.astype(jnp.bfloat16), ('attn', 'mb'), scat...]
    pallas_call x0 -> x1, Pallas kernels: none -> 95 us  [per_device(): pl.pallas_call(kernel, name='expert_block', out_shape=jax.ShapeDtypeStruc...]
    dot_general x5 -> x0, matrix products: 36.1 us -> none  [the longest x1 20 us: apply_experts(): jnp.einsum('gjcf,jfd->gjcd', hidden, w_down, preferred_element_type=jnp.f...]
    reduce_sum x3 -> x0, other arithmetic: 8.37 us -> none  [the longest x1 6.66 us: per_device(): total = jnp.sum(pair_weights[:, :, None] * picked, axis=1)]
    reshape x3 -> x1, local copies, waits for them, and re-layouts: 9.64 us -> 1.32 us  [per_device(): norm_gain.reshape(1, D)]
    convert_element_type x4 -> x0, other arithmetic: 3.2 us -> none  [the longest x1 1.38 us: per_device(): (floats * scale * norm_gain.astype(jnp.float32)).astype(jnp.bfloat16)]
  transfers between devices with their start and end apart: 3 -> 0, of which waited for: 3 -> 0; matrix products, arithmetic and copies ran while one was open for 1% -> 0% of each run, Pallas kernels for 0% -> 0%
where the time goes in v1:
time: 100 us; the launch traced here: 99.8 us
  Pallas kernels  95 us (95%)
  local copies, waits for them, and re-layouts  4.76 us (5%)
    pallas_call x1, Pallas kernels, per_device(): pl.pallas_call(kernel, name='expert_block', out_shape=jax.ShapeDtypeStruc...  95 us
    unnamed x2, local copies, waits for them, and re-layouts  3.44 us

profile of v1, /device:TPU:2, one launch (start us, length us, event | category | flops | bytes accessed | tf_op | source)
XLA Modules:
  0.0 99.8 jit_solution(2026182789909877357)
XLA Ops:
  0.0 1.3 %reshape.3.gain = bf16[1,6144]{1,0:T(2,128)(2,1)} reshape(bf16[6144]{0:T(1024)(128)(2,1)} %param.8) | data formatting | bytes 24576 | tf_op jit(solution)/shard_map/reshape | solution.py:438
  1.3 1.4 %copy.8.ids = s32[64,2]{1,0:T(8,128)} copy(s32[64,2]{0,1:T(2,128)} %param.10) | data formatting | bytes 1024 | tf_op args[3]
  2.7 95.0 %expert_block.1 = bf16[64,6144]{1,0:T(8,128)(2,1)} custom-call(bf16[64,6144]{1,0:T(8,128)(2,1)} %resid_h.1, bf16[1,6144]{1,0:T(2,128)(2,1)} %reshape.3.gain, bf16[8,6144]{1,0:T(8,128)(2,1)} %bitcast.2, s32[64,2]{1,0:T(8,128)} %copy.8.ids, s32[2,64]{1,0:T(2,128)} %bitcast.3, bf16[1,6144,256]{2,1,0:T(8,128)(2,1)} %wg_h.1, bf16[1,6144,256]{2,1,0:T(8,128)(2,1)} %wu_h.1, ...), custom_call_target="tpu_custom_call" | custom-call | tf_op jit(solution)/shard_map/expert_block/pallas_call | solution.py:392
  97.7 2.1 %copy.10 = bf16[64,6144]{1,0:T(8,128)(2,1)} copy(bf16[64,6144]{1,0:T(8,128)(2,1)} %expert_block.1) | data formatting | bytes 1572864

commit v2 on v1

v2 whole, which is shorter than its diff:
```python
import jax
import jax.numpy as jnp
from jax import lax
from jax.experimental import pallas as pl
from jax.experimental.pallas import tpu as pltpu
from jax.sharding import PartitionSpec as P

EXPERTS = 8
CAP = 24
ROWS = 64
D = 6144
HALF = D // 2
F = 256
SIDE = 4
LAYERS = 8
CHUNKS = 6
CW = D // CHUNKS
HW = CW // 2
OW = CW // LAYERS
LAGS = (0, 1, 2, 3, 4, 5)
ORDER = (
    (0, 0), (1, 0), (3, 0), (0, 1), (0, 3), (2, 0),
    (0, 2), (1, 1), (1, 3), (3, 1),
    (3, 3), (2, 1), (2, 3), (1, 2), (3, 2), (2, 2),
)
GROUPS = ((0, 6), (6, 10), (10, 16))
AT = {pair: n for n, pair in enumerate(ORDER)}
MESH = pl.DeviceIdType.MESH
BF = jnp.bfloat16
F32 = jnp.float32


def dot(a, b):
    return jnp.dot(a, b, preferred_element_type=F32)


def kernel(
    resid_h, gain_h, router_h, ids_h, wg_h, wu_h, wd_h, out_h,
    res, gain, router_t, ids, rows, wg, wu, wd, hid,
    p0, p1, p3, t1, t2, t3, qh, qf,
    v0, sp, pf,
    eo, ec, table, om,
    load_sem, sib_send, sib_recv, a_send, a_recv,
    b_send, qh_recv, qf_recv, pf_recv,
    e_recv, o_recv, out_sem,
):
    attn, z, c = lax.axis_index("attn"), lax.axis_index("exp"), lax.axis_index("mb")
    x, y = attn // SIDE, attn % SIDE

    def plane(dx, dy):
        return {"attn": ((x + dx) % SIDE) * SIDE + (y + dy) % SIDE, "exp": z, "mb": c}

    def on_p(d):
        d = d % SIDE
        return plane((1 - c) * d, c * d)

    def on_q(d):
        d = d % SIDE
        return plane(c * d, (1 - c) * d)

    def on_z(d):
        return {"attn": attn, "exp": (z + d) % LAYERS, "mb": c}

    sibling = {"attn": attn, "exp": z, "mb": 1 - c}

    barrier = pltpu.get_barrier_semaphore()
    partners = [on_p(1), on_p(-1), on_q(1), on_q(-1), sibling, on_p(2)]
    partners += [on_z(d) for d in range(1, LAYERS)]
    for device in partners:
        pl.semaphore_signal(barrier, inc=1, device_id=device, device_id_type=MESH)

    pairs = (
        (ids_h, ids), (resid_h, res), (gain_h, gain), (router_h, router_t),
        (wg_h.at[0], wg.at[0]), (wu_h.at[0], wu.at[0]), (wd_h.at[0], wd.at[0]),
    )
    loads = [pltpu.make_async_copy(src, dst, load_sem.at[i]) for i, (src, dst) in enumerate(pairs)]
    for load in loads:
        load.start()

    loads[0].wait()
    hit = ((ids[0:1, :] == z) | (ids[1:2, :] == z)).astype(F32)
    earlier = (
        lax.broadcasted_iota(jnp.int32, (ROWS, ROWS), 0)
        < lax.broadcasted_iota(jnp.int32, (ROWS, ROWS), 1)
    ).astype(F32).astype(BF)
    rank = dot(jnp.broadcast_to(hit, (8, ROWS)).astype(BF), earlier)[0:1, :]
    slot = lax.broadcasted_iota(jnp.int32, (CAP, ROWS), 0).astype(F32)
    pick = jnp.where((rank == slot) & (hit > 0.5), 1.0, 0.0).astype(BF)

    loads[1].wait()
    square = jnp.zeros((CAP, CW), F32)
    for k in range(CHUNKS):
        cols = pl.ds(k * CW, CW)
        part = dot(pick, res[:, cols])
        rows[0, :, cols] = part.astype(BF)
        square = square + part * part
    scale = lax.rsqrt(jnp.sum(square, axis=1, keepdims=True) / D + 1e-05)
    loads[2].wait()

    def gained(k):
        return gain[pl.ds(k * CW, CW)].astype(F32).reshape(1, CW)

    for k in range(CHUNKS):
        cols = pl.ds(k * CW, CW)
        part = rows[0, :, cols].astype(F32)
        rows[0, :, cols] = (part * scale * gained(k)).astype(BF)

    pl.semaphore_wait(barrier, len(partners))

    def remote(src, dst, send, recv, device):
        return pltpu.make_async_remote_copy(
            src_ref=src, dst_ref=dst, send_sem=send, recv_sem=recv,
            device_id=device, device_id_type=MESH,
        )

    def block(pr, qr, half=None):
        ref = rows.at[AT[pr, qr]]
        return ref if half is None else ref.at[:, pl.ds(half * HALF, HALF)]

    def a_copy(pr, qr, to_pr, to_qr, half, device):
        along_q = qr != to_qr
        remote(
            block(pr, qr, half), block(to_pr, to_qr, half),
            a_send.at[int(along_q)], a_recv.at[AT[to_pr, to_qr]], device,
        ).start()

    def a_wait(pr, qr):
        ref = block(pr, qr)
        remote(ref, ref, a_send.at[0], a_recv.at[AT[pr, qr]], sibling).wait_recv()

    a_copy(0, 0, 3, 0, None, on_p(1))
    a_copy(0, 0, 1, 0, None, on_p(-1))
    a_copy(0, 0, 0, 3, None, on_q(1))
    a_copy(0, 0, 0, 1, None, on_q(-1))

    siblings = []
    for i, (src, dst) in enumerate(((wg_h, wg), (wu_h, wu), (wd_h, wd))):
        copy = remote(src.at[0], dst.at[1], sib_send.at[i], sib_recv.at[i], sibling)
        copy.start()
        siblings.append(copy)

    square = jnp.zeros((ROWS, CW), F32)
    for k in range(CHUNKS):
        part = res[:, pl.ds(k * CW, CW)].astype(F32)
        square = square + part * part
    scale = lax.rsqrt(jnp.sum(square, axis=1, keepdims=True) / D + 1e-05)
    logits = jnp.zeros((ROWS, EXPERTS), F32)
    loads[3].wait()
    for k in range(CHUNKS):
        cols = pl.ds(k * CW, CW)
        normed = (res[:, cols].astype(F32) * scale * gained(k)).astype(BF)
        logits = logits + lax.dot_general(
            normed, router_t[:, cols], (((1,), (1,)), ((), ())), preferred_element_type=F32
        )
    expert = lax.broadcasted_iota(jnp.int32, (ROWS, EXPERTS), 1)
    unit = (
        lax.broadcasted_iota(jnp.int32, (ROWS, ROWS), 0)
        == lax.broadcasted_iota(jnp.int32, (ROWS, ROWS), 1)
    ).astype(F32).astype(BF)

    def upright(row):
        turned = lax.dot_general(
            unit, jnp.broadcast_to(row.astype(F32), (EXPERTS, ROWS)).astype(BF),
            (((1,), (1,)), ((), ())), preferred_element_type=F32,
        )
        return turned[:, 0:1].astype(jnp.int32)

    id_a, id_b = upright(ids[0:1, :]), upright(ids[1:2, :])
    near = (expert + z) % EXPERTS
    chose_a, chose_b = near == id_a, near == id_b
    chosen = jnp.where(chose_a | chose_b, 1.0, 0.0)
    lower = (
        lax.broadcasted_iota(jnp.int32, (ROWS, ROWS), 0)
        > lax.broadcasted_iota(jnp.int32, (ROWS, ROWS), 1)
    ).astype(F32).astype(BF)
    ranks = dot(lower, chosen.astype(BF))
    of_a = jnp.sum(jnp.where(expert == id_a, logits, 0.0), axis=1, keepdims=True)
    of_b = jnp.sum(jnp.where(expert == id_b, logits, 0.0), axis=1, keepdims=True)
    first, second = jax.nn.sigmoid(of_a - of_b), jax.nn.sigmoid(of_b - of_a)
    weight = jnp.where(chose_a, first, 0.0) + jnp.where(chose_b, second, 0.0)
    weight_hi = weight.astype(BF)
    weight_lo = (weight - weight_hi.astype(F32)).astype(BF)
    wide = EXPERTS * CAP
    start = lax.broadcasted_iota(jnp.int32, (EXPERTS, wide), 0) * CAP
    lane = lax.broadcasted_iota(jnp.int32, (EXPERTS, wide), 1)
    spread = jnp.where((lane >= start) & (lane < start + CAP), 1.0, 0.0).astype(BF)
    place = (lax.broadcasted_iota(jnp.int32, (ROWS, wide), 1) % CAP).astype(F32)
    here = (dot(ranks.astype(BF), spread) == place) & (dot(chosen.astype(BF), spread) > 0.5)
    table[0:ROWS, :] = jnp.where(here, dot(weight_hi, spread), 0.0).astype(BF)
    table[ROWS:, :] = jnp.where(here, dot(weight_lo, spread), 0.0).astype(BF)

    def hidden(group, s):
        low, high = GROUPS[group]
        lhs = rows[low:high].reshape((high - low) * CAP, D)
        gate = dot(lhs, wg[s])
        upper = dot(lhs, wu[s])
        value = gate / (1.0 + jnp.exp(-gate)) * upper
        hid[low * CAP : high * CAP, s * F : (s + 1) * F] = value.astype(BF)

    def forward_q(pr):
        a_wait(pr, 1)
        a_copy(pr, 1, pr, 2, 0, on_q(-1))
        a_wait(pr, 3)
        a_copy(pr, 3, pr, 2, 1, on_q(1))

    def spread_q(pr):
        a_copy(pr, 0, pr, 3, None, on_q(1))
        a_copy(pr, 0, pr, 1, None, on_q(-1))

    a_wait(1, 0)
    a_copy(1, 0, 2, 0, 0, on_p(-1))
    a_wait(3, 0)
    a_copy(3, 0, 2, 0, 1, on_p(1))
    forward_q(0)
    spread_q(1)
    spread_q(3)
    a_wait(2, 0)
    spread_q(2)
    loads[4].wait()
    loads[5].wait()
    hidden(0, 0)
    a_wait(0, 2)
    forward_q(1)
    siblings[0].wait_recv()
    siblings[1].wait_recv()
    hidden(0, 1)
    forward_q(3)
    hidden(1, 0)
    hidden(1, 1)
    forward_q(2)
    a_wait(1, 2)
    a_wait(3, 2)
    a_wait(2, 2)
    hidden(2, 0)
    hidden(2, 1)
    loads[6].wait()
    siblings[2].wait_recv()
    for copy in siblings:
        copy.wait_send()
    for along_q, ref in enumerate((rows.at[0:3], rows.at[0:12])):
        remote(ref, ref, a_send.at[along_q], a_recv.at[0], sibling).wait_send()

    def ds_full(k):
        return pl.ds(pl.multiple_of(k * CW, CW), CW)

    def ds_half(k, half):
        return pl.ds(pl.multiple_of(k * CW + half * HW, HW), HW)

    def ds_pack(k):
        return pl.ds(pl.multiple_of(k * HW, HW), HW)

    def ds_own(k):
        return pl.ds(pl.multiple_of(k * OW, OW), OW)

    def ds_layer(k, layer):
        return pl.ds(pl.multiple_of(k * CW + layer * OW, OW), OW)

    def q_half(k, side):
        return remote(
            t2.at[:, :, ds_half(k, side)], qh.at[side, :, :, ds_pack(k)],
            b_send.at[0], qh_recv.at[k], on_q(1 - 2 * side),
        )

    def q_full(k, side):
        return remote(
            (t1, t3)[side].at[:, :, ds_full(k)], qf.at[side, :, :, ds_full(k)],
            b_send.at[1], qf_recv.at[k], on_q(1 - 2 * side),
        )

    def p_copy(k, d):
        return remote(
            sp.at[d - 1, :, ds_full(k)], pf.at[SIDE - 1 - d, :, ds_full(k)],
            b_send.at[2], pf_recv.at[k], on_p(d),
        )

    def e_copy(k, d):
        return remote(
            eo.at[:, ds_layer(k, (z + d) % LAYERS)], ec.at[LAYERS - d, :, ds_own(k)],
            b_send.at[3], e_recv.at[k], on_z(d),
        )

    def o_copy(k, d):
        mine = om.at[:, ds_layer(k, z)]
        return remote(mine, mine, b_send.at[4], o_recv.at[k], on_z(d))

    def arrived(ref, sem):
        remote(ref, ref, b_send.at[0], sem, sibling).wait_recv()

    def left(ref, n):
        remote(ref, ref, b_send.at[n], out_sem.at[0], sibling).wait_send()

    def stage_down(k):
        cols = ds_full(k)
        value = dot(hid[:, 0:F], wd[0, :, cols]) + dot(hid[:, F:], wd[1, :, cols])
        value = value.reshape(SIDE * SIDE, CAP, CW)
        for pr in range(SIDE):
            t2[pr, :, cols] = value[AT[pr, 2]].astype(BF)
        q_half(k, 0).start()
        q_half(k, 1).start()
        for pr in range(SIDE):
            p0[pr, :, cols] = value[AT[pr, 0]]
            p1[pr, :, cols] = value[AT[pr, 1]]
            p3[pr, :, cols] = value[AT[pr, 3]]

    def stage_q_half(k):
        low, high, pack = ds_half(k, 0), ds_half(k, 1), ds_pack(k)
        arrived(qh.at[:, :, :, pack], qh_recv.at[k])
        t1[:, :, low] = (p1[:, :, low] + qh[0, :, :, pack].astype(F32)).astype(BF)
        t1[:, :, high] = p1[:, :, high].astype(BF)
        q_full(k, 0).start()
        t3[:, :, low] = p3[:, :, low].astype(BF)
        t3[:, :, high] = (p3[:, :, high] + qh[1, :, :, pack].astype(F32)).astype(BF)
        q_full(k, 1).start()

    def stage_q_full(k):
        cols = ds_full(k)
        arrived(qf.at[:, :, :, cols], qf_recv.at[k])

        def summed(pr):
            return p0[pr, :, cols] + qf[0, pr, :, cols].astype(F32) + qf[1, pr, :, cols].astype(F32)

        for d in (2, 1, 3):
            sp[d - 1, :, cols] = summed(d).astype(BF)
            p_copy(k, d).start()
        v0[:, cols] = summed(0)

    def stage_p(k):
        cols = ds_full(k)
        arrived(pf.at[:, :, cols], pf_recv.at[k])
        total = v0[:, cols]
        for n in range(SIDE - 1):
            total = total + pf[n, :, cols].astype(F32)
        eo[:, cols] = total.astype(BF)
        for d in range(1, LAYERS):
            e_copy(k, d).start()

    def stage_mix(k):
        mine = ds_layer(k, z)
        ec[0, :, ds_own(k)] = eo[:, mine]
        arrived(ec.at[1:LAYERS, :, ds_own(k)], e_recv.at[k])
        every = ec[:, :, ds_own(k)].astype(F32).reshape(LAYERS * CAP, OW).astype(BF)
        both = dot(table[...], every)
        om[:, mine] = (res[:, mine].astype(F32) + (both[:ROWS] + both[ROWS:])).astype(BF)
        for d in range(1, LAYERS):
            o_copy(k, d).start()

    def out_copy(k):
        return pltpu.make_async_copy(om.at[:, ds_full(k)], out_h.at[:, ds_full(k)], out_sem.at[0])

    def stage_out(k):
        arrived(om.at[:, pl.ds(pl.multiple_of(k * CW, CW), (LAYERS - 1) * OW)], o_recv.at[k])
        out_copy(k).start()

    stages = [stage_down, stage_q_half, stage_q_full, stage_p, stage_mix, stage_out]

    def step(i, carry):
        for s, stage in enumerate(stages):
            lag = LAGS[s]

            @pl.when((i >= lag) & (i < lag + CHUNKS))
            def _(lag=lag, stage=stage):
                stage(i - lag)
        return carry

    lax.fori_loop(0, CHUNKS + LAGS[-1], step, 0)

    left(t2, 0)
    left(qf, 1)
    left(pf, 2)
    left(ec.at[1:LAYERS], 3)
    left(om.at[:, 0 : (LAYERS - 1) * OW * CHUNKS], 4)
    pltpu.make_async_copy(om, out_h, out_sem.at[0]).wait()


def per_device(resid, norm_gain, router, expert_ids, w_gate, w_up, w_down):
    hbm = pl.BlockSpec(memory_space=pl.ANY)
    dma = pltpu.SemaphoreType.DMA
    block = (SIDE, CAP, D)
    return pl.pallas_call(
        kernel,
        name="expert_block",
        out_shape=jax.ShapeDtypeStruct((ROWS, D), BF),
        in_specs=[hbm] * 7,
        out_specs=hbm,
        scratch_shapes=[
            pltpu.VMEM((ROWS, D), BF),
            pltpu.VMEM((D,), BF),
            pltpu.VMEM((EXPERTS, D), BF),
            pltpu.VMEM((2, ROWS), jnp.int32),
            pltpu.VMEM((SIDE * SIDE, CAP, D), BF),
            pltpu.VMEM((2, D, F), BF),
            pltpu.VMEM((2, D, F), BF),
            pltpu.VMEM((2, F, D), BF),
            pltpu.VMEM((SIDE * SIDE * CAP, 2 * F), BF),
            pltpu.VMEM(block, F32),
            pltpu.VMEM(block, F32),
            pltpu.VMEM(block, F32),
            pltpu.VMEM(block, BF),
            pltpu.VMEM(block, BF),
            pltpu.VMEM(block, BF),
            pltpu.VMEM((2, SIDE, CAP, HALF), BF),
            pltpu.VMEM((2, SIDE, CAP, D), BF),
            pltpu.VMEM((CAP, D), F32),
            pltpu.VMEM((SIDE - 1, CAP, D), BF),
            pltpu.VMEM((SIDE - 1, CAP, D), BF),
            pltpu.VMEM((CAP, D), BF),
            pltpu.VMEM((LAYERS, CAP, D // LAYERS), BF),
            pltpu.VMEM((2 * ROWS, EXPERTS * CAP), BF),
            pltpu.VMEM((ROWS, D), BF),
            dma((7,)),
            dma((3,)),
            dma((3,)),
            dma((2,)),
            dma((SIDE * SIDE,)),
            dma((5,)),
        ]
        + [dma((CHUNKS,))] * 5
        + [dma((1,))],
        compiler_params=pltpu.CompilerParams(
            collective_id=0, has_side_effects=True, vmem_limit_bytes=60 * 1024 * 1024
        ),
    )(
        resid, norm_gain, router.T, expert_ids.T, w_gate, w_up, w_down
    )


def solution(mesh):
    in_specs = (
        P(("attn", "mb"), None),
        P(),
        P(),
        P(("attn", "mb"), None),
        P("exp", None, ("attn", "mb")),
        P("exp", None, ("attn", "mb")),
        P("exp", ("attn", "mb"), None),
    )
    out_specs = P(("attn", "mb"), None)
    return jax.shard_map(
        per_device, mesh=mesh, in_specs=in_specs, out_specs=out_specs, check_vma=False
    )
```

time: 100 us -> 90.4 us (0.904)
  Pallas kernels: 95 us -> 88.2 us
  local copies, waits for them, and re-layouts: 4.76 us -> 2.06 us
    pallas_call x1, Pallas kernels: 95 us -> 88.2 us  [per_device(): pl.pallas_call(kernel, name='expert_block', out_shape=jax.ShapeDtypeStruc...]
    unnamed x2 -> x1, local copies, waits for them, and re-layouts: 3.44 us -> 2.06 us
    reshape x1 -> x0, local copies, waits for them, and re-layouts: 1.32 us -> none  [per_device(): norm_gain.reshape(1, D)]
where the time goes in v2:
time: 90.4 us; the launch traced here: 90.3 us
  Pallas kernels  88.2 us (98%)
  local copies, waits for them, and re-layouts  2.06 us (2%)
    pallas_call x1, Pallas kernels, per_device(): pl.pallas_call(kernel, name='expert_block', out_shape=jax.ShapeDtypeStruc...  88.2 us
    unnamed x1, local copies, waits for them, and re-layouts  2.06 us

profile of v2, /device:TPU:2, one launch (start us, length us, event | category | flops | bytes accessed | tf_op | source)
XLA Modules:
  0.0 90.3 jit_solution(1494647175126411920)
XLA Ops:
  0.0 88.2 %expert_block.1 = bf16[64,6144]{1,0:T(8,128)(2,1)} custom-call(bf16[64,6144]{1,0:T(8,128)(2,1)} %resid_h.1, bf16[6144]{0:T(1024)(128)(2,1)} %gain_h.1, bf16[8,6144]{1,0:T(8,128)(2,1)} %bitcast.2, s32[2,64]{1,0:T(2,128)} %bitcast.3, bf16[1,6144,256]{2,1,0:T(8,128)(2,1)} %wg_h.1, bf16[1,6144,256]{2,1,0:T(8,128)(2,1)} %wu_h.1, bf16[1,256,6144]{2,1,0:T(8,128)(2,1)} %wd_h.1), custom_call_target="tpu_custom_call" | custom-call | tf_op jit(solution)/shard_map/expert_block/pallas_call | solution.py:379
  88.2 2.1 %copy.9 = bf16[64,6144]{1,0:T(8,128)(2,1)} copy(bf16[64,6144]{1,0:T(8,128)(2,1)} %expert_block.1) | data formatting | bytes 1572864

commit v3 on v2

--- a/solution.py
+++ b/solution.py
@@ -18,6 +18,8 @@
 HW = CW // 2
 OW = CW // LAYERS
 LAGS = (0, 1, 2, 3, 4, 5)
+LAST = CHUNKS - 1
+FAR_FIRST = (4, 3, 5, 2, 6, 1, 7)
 ORDER = (
     (0, 0), (1, 0), (3, 0), (0, 1), (0, 3), (2, 0),
     (0, 2), (1, 1), (1, 3), (3, 1),
@@ -37,7 +39,7 @@
 def kernel(
     resid_h, gain_h, router_h, ids_h, wg_h, wu_h, wd_h, out_h,
     res, gain, router_t, ids, rows, wg, wu, wd, hid,
-    p0, p1, p3, t1, t2, t3, qh, qf,
+    p0, p1, p3, t1, t2, t3, qh, qf, qd,
     v0, sp, pf,
     eo, ec, table, om,
     load_sem, sib_send, sib_recv, a_send, a_recv,
@@ -64,7 +66,7 @@
     sibling = {"attn": attn, "exp": z, "mb": 1 - c}
 
     barrier = pltpu.get_barrier_semaphore()
-    partners = [on_p(1), on_p(-1), on_q(1), on_q(-1), sibling, on_p(2)]
+    partners = [on_p(1), on_p(-1), on_q(1), on_q(-1), sibling, on_p(2), on_q(2)]
     partners += [on_z(d) for d in range(1, LAYERS)]
     for device in partners:
         pl.semaphore_signal(barrier, inc=1, device_id=device, device_id_type=MESH)
@@ -113,25 +115,25 @@
             device_id=device, device_id_type=MESH,
         )
 
-    def block(pr, qr, half=None):
-        ref = rows.at[AT[pr, qr]]
-        return ref if half is None else ref.at[:, pl.ds(half * HALF, HALF)]
-
-    def a_copy(pr, qr, to_pr, to_qr, half, device):
+    def block(pr, qr, half):
+        return rows.at[AT[pr, qr], :, pl.ds(half * HALF, HALF)]
+
+    def a_copy(pr, qr, half, to_pr, to_qr, device):
         along_q = qr != to_qr
         remote(
             block(pr, qr, half), block(to_pr, to_qr, half),
-            a_send.at[int(along_q)], a_recv.at[AT[to_pr, to_qr]], device,
+            a_send.at[int(along_q)], a_recv.at[AT[to_pr, to_qr], half], device,
         ).start()
 
-    def a_wait(pr, qr):
-        ref = block(pr, qr)
-        remote(ref, ref, a_send.at[0], a_recv.at[AT[pr, qr]], sibling).wait_recv()
-
-    a_copy(0, 0, 3, 0, None, on_p(1))
-    a_copy(0, 0, 1, 0, None, on_p(-1))
-    a_copy(0, 0, 0, 3, None, on_q(1))
-    a_copy(0, 0, 0, 1, None, on_q(-1))
+    def a_wait(pr, qr, half):
+        ref = block(pr, qr, half)
+        remote(ref, ref, a_send.at[0], a_recv.at[AT[pr, qr], half], sibling).wait_recv()
+
+    for first in (0, 1):
+        a_copy(0, 0, first, 1, 0, on_p(-1))
+        a_copy(0, 0, 1 - first, 3, 0, on_p(1))
+        a_copy(0, 0, first, 0, 1, on_q(-1))
+        a_copy(0, 0, 1 - first, 0, 3, on_q(1))
 
     siblings = []
     for i, (src, dst) in enumerate(((wg_h, wg), (wu_h, wu), (wd_h, wd))):
@@ -198,39 +200,50 @@
         hid[low * CAP : high * CAP, s * F : (s + 1) * F] = value.astype(BF)
 
     def forward_q(pr):
-        a_wait(pr, 1)
-        a_copy(pr, 1, pr, 2, 0, on_q(-1))
-        a_wait(pr, 3)
-        a_copy(pr, 3, pr, 2, 1, on_q(1))
-
-    def spread_q(pr):
-        a_copy(pr, 0, pr, 3, None, on_q(1))
-        a_copy(pr, 0, pr, 1, None, on_q(-1))
-
-    a_wait(1, 0)
-    a_copy(1, 0, 2, 0, 0, on_p(-1))
-    a_wait(3, 0)
-    a_copy(3, 0, 2, 0, 1, on_p(1))
+        a_wait(pr, 1, 0)
+        a_copy(pr, 1, 0, pr, 2, on_q(-1))
+        a_wait(pr, 3, 1)
+        a_copy(pr, 3, 1, pr, 2, on_q(1))
+
+    def spread_q(pr, half):
+        for side in (half, 1 - half):
+            a_copy(pr, 0, half, pr, 1 + 2 * side, on_q(2 * side - 1))
+
+    def a_rest(*blocks):
+        for pr, qr, half in blocks:
+            a_wait(pr, qr, half)
+
+    a_wait(1, 0, 0)
+    a_copy(1, 0, 0, 2, 0, on_p(-1))
+    a_wait(3, 0, 1)
+    a_copy(3, 0, 1, 2, 0, on_p(1))
     forward_q(0)
-    spread_q(1)
-    spread_q(3)
-    a_wait(2, 0)
-    spread_q(2)
+    spread_q(1, 0)
+    spread_q(3, 1)
+    a_wait(1, 0, 1)
+    spread_q(1, 1)
+    a_wait(3, 0, 0)
+    spread_q(3, 0)
+    a_wait(2, 0, 0)
+    spread_q(2, 0)
+    a_wait(2, 0, 1)
+    spread_q(2, 1)
     loads[4].wait()
     loads[5].wait()
+    a_rest((0, 1, 1), (0, 3, 0))
     hidden(0, 0)
-    a_wait(0, 2)
     forward_q(1)
     siblings[0].wait_recv()
     siblings[1].wait_recv()
     hidden(0, 1)
     forward_q(3)
+    a_rest((0, 2, 0), (0, 2, 1), (1, 1, 1), (1, 3, 0), (3, 1, 1))
     hidden(1, 0)
+    forward_q(2)
     hidden(1, 1)
-    forward_q(2)
-    a_wait(1, 2)
-    a_wait(3, 2)
-    a_wait(2, 2)
+    a_rest((3, 3, 0), (2, 1, 1), (2, 3, 0))
+    for pr in (1, 3, 2):
+        a_rest((pr, 2, 0), (pr, 2, 1))
     hidden(2, 0)
     hidden(2, 1)
     loads[6].wait()
@@ -238,7 +251,7 @@
     for copy in siblings:
         copy.wait_send()
     for along_q, ref in enumerate((rows.at[0:3], rows.at[0:12])):
-        remote(ref, ref, a_send.at[along_q], a_recv.at[0], sibling).wait_send()
+        remote(ref, ref, a_send.at[along_q], a_recv.at[0, 0], sibling).wait_send()
 
     def ds_full(k):
         return pl.ds(pl.multiple_of(k * CW, CW), CW)
@@ -265,6 +278,14 @@
         return remote(
             (t1, t3)[side].at[:, :, ds_full(k)], qf.at[side, :, :, ds_full(k)],
             b_send.at[1], qf_recv.at[k], on_q(1 - 2 * side),
+        )
+
+    def at_end(k):
+        return (k == 0) | (k == LAST)
+
+    def q_direct(k):
+        return remote(
+            t2.at[:, :, ds_full(k)], qd.at[k // LAST], b_send.at[0], qh_recv.at[k], on_q(2)
         )
 
     def p_copy(k, d):
@@ -295,26 +316,51 @@
         value = value.reshape(SIDE * SIDE, CAP, CW)
         for pr in range(SIDE):
             t2[pr, :, cols] = value[AT[pr, 2]].astype(BF)
-        q_half(k, 0).start()
-        q_half(k, 1).start()
+
+        @pl.when(at_end(k))
+        def _():
+            q_direct(k).start()
+
+        @pl.when(jnp.logical_not(at_end(k)))
+        def _():
+            q_half(k, 0).start()
+            q_half(k, 1).start()
+
+        for pr in range(SIDE):
+            p1[pr, :, cols] = value[AT[pr, 1]]
+            p3[pr, :, cols] = value[AT[pr, 3]]
+
+        @pl.when(at_end(k))
+        def _():
+            t1[:, :, cols] = p1[:, :, cols].astype(BF)
+            q_full(k, 0).start()
+            t3[:, :, cols] = p3[:, :, cols].astype(BF)
+            q_full(k, 1).start()
+
         for pr in range(SIDE):
             p0[pr, :, cols] = value[AT[pr, 0]]
-            p1[pr, :, cols] = value[AT[pr, 1]]
-            p3[pr, :, cols] = value[AT[pr, 3]]
 
     def stage_q_half(k):
         low, high, pack = ds_half(k, 0), ds_half(k, 1), ds_pack(k)
-        arrived(qh.at[:, :, :, pack], qh_recv.at[k])
-        t1[:, :, low] = (p1[:, :, low] + qh[0, :, :, pack].astype(F32)).astype(BF)
-        t1[:, :, high] = p1[:, :, high].astype(BF)
-        q_full(k, 0).start()
-        t3[:, :, low] = p3[:, :, low].astype(BF)
-        t3[:, :, high] = (p3[:, :, high] + qh[1, :, :, pack].astype(F32)).astype(BF)
-        q_full(k, 1).start()
+
+        @pl.when(jnp.logical_not(at_end(k)))
+        def _():
+            arrived(qh.at[:, :, :, pack], qh_recv.at[k])
+            t1[:, :, low] = (p1[:, :, low] + qh[0, :, :, pack].astype(F32)).astype(BF)
+            t1[:, :, high] = p1[:, :, high].astype(BF)
+            q_full(k, 0).start()
+            t3[:, :, low] = p3[:, :, low].astype(BF)
+            t3[:, :, high] = (p3[:, :, high] + qh[1, :, :, pack].astype(F32)).astype(BF)
+            q_full(k, 1).start()
 
     def stage_q_full(k):
         cols = ds_full(k)
         arrived(qf.at[:, :, :, cols], qf_recv.at[k])
+
+        @pl.when(at_end(k))
+        def _():
+            arrived(qd.at[0], qh_recv.at[k])
+            p0[:, :, cols] = p0[:, :, cols] + qd[k // LAST].astype(F32)
 
         def summed(pr):
             return p0[pr, :, cols] + qf[0, pr, :, cols].astype(F32) + qf[1, pr, :, cols].astype(F32)
@@ -331,7 +377,7 @@
         for n in range(SIDE - 1):
             total = total + pf[n, :, cols].astype(F32)
         eo[:, cols] = total.astype(BF)
-        for d in range(1, LAYERS):
+        for d in FAR_FIRST:
             e_copy(k, d).start()
 
     def stage_mix(k):
@@ -341,7 +387,7 @@
         every = ec[:, :, ds_own(k)].astype(F32).reshape(LAYERS * CAP, OW).astype(BF)
         both = dot(table[...], every)
         om[:, mine] = (res[:, mine].astype(F32) + (both[:ROWS] + both[ROWS:])).astype(BF)
-        for d in range(1, LAYERS):
+        for d in FAR_FIRST:
             o_copy(k, d).start()
 
     def out_copy(k):
@@ -357,12 +403,21 @@
         for s, stage in enumerate(stages):
             lag = LAGS[s]
 
-            @pl.when((i >= lag) & (i < lag + CHUNKS))
-            def _(lag=lag, stage=stage):
-                stage(i - lag)
+            if s < 2:
+                @pl.when((i >= lag) & (i < lag + CHUNKS))
+                def _(lag=lag, stage=stage):
+                    stage(i - lag)
+            else:
+                @pl.when((i >= lag) & (i < lag + LAST))
+                def _(lag=lag, stage=stage):
+                    stage(i - lag)
+
+                @pl.when(i == lag + LAST - 1)
+                def _(stage=stage):
+                    stage(LAST)
         return carry
 
-    lax.fori_loop(0, CHUNKS + LAGS[-1], step, 0)
+    lax.fori_loop(0, LAST + LAGS[-1], step, 0)
 
     left(t2, 0)
     left(qf, 1)
@@ -400,6 +455,7 @@
             pltpu.VMEM(block, BF),
             pltpu.VMEM((2, SIDE, CAP, HALF), BF),
             pltpu.VMEM((2, SIDE, CAP, D), BF),
+            pltpu.VMEM((2, SIDE, CAP, CW), BF),
             pltpu.VMEM((CAP, D), F32),
             pltpu.VMEM((SIDE - 1, CAP, D), BF),
             pltpu.VMEM((SIDE - 1, CAP, D), BF),
@@ -411,7 +467,7 @@
             dma((3,)),
             dma((3,)),
             dma((2,)),
-            dma((SIDE * SIDE,)),
+            dma((SIDE * SIDE, 2)),
             dma((5,)),
         ]
         + [dma((CHUNKS,))] * 5

time: 90.4 us -> 87.1 us (0.963)
  Pallas kernels: 88.2 us -> 84.2 us
    pallas_call x1, Pallas kernels: 88.2 us -> 84.2 us  [per_device(): pl.pallas_call(kernel, name='expert_block', out_shape=jax.ShapeDtypeStruc...]
where the time goes in v3:
time: 87.1 us; the launch traced here: 86.3 us
  Pallas kernels  84.2 us (97%)
  local copies, waits for them, and re-layouts  2.06 us (2%)
    pallas_call x1, Pallas kernels, per_device(): pl.pallas_call(kernel, name='expert_block', out_shape=jax.ShapeDtypeStruc...  84.2 us
    unnamed x1, local copies, waits for them, and re-layouts  2.06 us

profile of v3, /device:TPU:2, one launch (start us, length us, event | category | flops | bytes accessed | tf_op | source)
XLA Modules:
  0.0 86.3 jit_solution(12227795560524562489)
XLA Ops:
  0.0 84.2 %expert_block.1 = bf16[64,6144]{1,0:T(8,128)(2,1)} custom-call(bf16[64,6144]{1,0:T(8,128)(2,1)} %resid_h.1, bf16[6144]{0:T(1024)(128)(2,1)} %gain_h.1, bf16[8,6144]{1,0:T(8,128)(2,1)} %bitcast.2, s32[2,64]{1,0:T(2,128)} %bitcast.3, bf16[1,6144,256]{2,1,0:T(8,128)(2,1)} %wg_h.1, bf16[1,6144,256]{2,1,0:T(8,128)(2,1)} %wu_h.1, bf16[1,256,6144]{2,1,0:T(8,128)(2,1)} %wd_h.1), custom_call_target="tpu_custom_call" | custom-call | tf_op jit(solution)/shard_map/expert_block/pallas_call | solution.py:434
  84.2 2.1 %copy.9 = bf16[64,6144]{1,0:T(8,128)(2,1)} copy(bf16[64,6144]{1,0:T(8,128)(2,1)} %expert_block.1) | data formatting | bytes 1572864

commit v4 on v3

--- a/solution.py
+++ b/solution.py
@@ -13,19 +13,28 @@
 F = 256
 SIDE = 4
 LAYERS = 8
-CHUNKS = 6
+PARTS = 6
+PW = D // PARTS
+CHUNKS = 12
 CW = D // CHUNKS
 HW = CW // 2
-OW = CW // LAYERS
-LAGS = (0, 1, 2, 3, 4, 5)
+OW = 128
+OWNERS = CW // OW
+TURNS = LAYERS // OWNERS
+LAGS = (0, 2, 4, 6, 8, 10, 16)
+RELAYED = CHUNKS - 2
 LAST = CHUNKS - 1
 FAR_FIRST = (4, 3, 5, 2, 6, 1, 7)
 ORDER = (
-    (0, 0), (1, 0), (3, 0), (0, 1), (0, 3), (2, 0),
-    (0, 2), (1, 1), (1, 3), (3, 1),
+    (0, 0), (0, 1), (0, 3), (0, 2),
+    (1, 0), (3, 0), (2, 0), (1, 1), (1, 3), (3, 1),
     (3, 3), (2, 1), (2, 3), (1, 2), (3, 2), (2, 2),
 )
-GROUPS = ((0, 6), (6, 10), (10, 16))
+GROUPS = ((0, 4), (4, 10), (10, 16))
+EARLY = 4 * CAP
+STEPS = (0, 1, 3, 2)
+EW = 2048
+SPAN = EW // CW
 AT = {pair: n for n, pair in enumerate(ORDER)}
 MESH = pl.DeviceIdType.MESH
 BF = jnp.bfloat16
@@ -44,7 +53,7 @@
     eo, ec, table, om,
     load_sem, sib_send, sib_recv, a_send, a_recv,
     b_send, qh_recv, qf_recv, pf_recv,
-    e_recv, o_recv, out_sem,
+    e_recv, o_recv, early_recv, out_sem,
 ):
     attn, z, c = lax.axis_index("attn"), lax.axis_index("exp"), lax.axis_index("mb")
     x, y = attn // SIDE, attn % SIDE
@@ -90,9 +99,9 @@
     pick = jnp.where((rank == slot) & (hit > 0.5), 1.0, 0.0).astype(BF)
 
     loads[1].wait()
-    square = jnp.zeros((CAP, CW), F32)
-    for k in range(CHUNKS):
-        cols = pl.ds(k * CW, CW)
+    square = jnp.zeros((CAP, PW), F32)
+    for k in range(PARTS):
+        cols = pl.ds(k * PW, PW)
         part = dot(pick, res[:, cols])
         rows[0, :, cols] = part.astype(BF)
         square = square + part * part
@@ -100,10 +109,10 @@
     loads[2].wait()
 
     def gained(k):
-        return gain[pl.ds(k * CW, CW)].astype(F32).reshape(1, CW)
-
-    for k in range(CHUNKS):
-        cols = pl.ds(k * CW, CW)
+        return gain[pl.ds(k * PW, PW)].astype(F32).reshape(1, PW)
+
+    for k in range(PARTS):
+        cols = pl.ds(k * PW, PW)
         part = rows[0, :, cols].astype(F32)
         rows[0, :, cols] = (part * scale * gained(k)).astype(BF)
 
@@ -141,15 +150,15 @@
         copy.start()
         siblings.append(copy)
 
-    square = jnp.zeros((ROWS, CW), F32)
-    for k in range(CHUNKS):
-        part = res[:, pl.ds(k * CW, CW)].astype(F32)
+    square = jnp.zeros((ROWS, PW), F32)
+    for k in range(PARTS):
+        part = res[:, pl.ds(k * PW, PW)].astype(F32)
         square = square + part * part
     scale = lax.rsqrt(jnp.sum(square, axis=1, keepdims=True) / D + 1e-05)
     logits = jnp.zeros((ROWS, EXPERTS), F32)
     loads[3].wait()
-    for k in range(CHUNKS):
-        cols = pl.ds(k * CW, CW)
+    for k in range(PARTS):
+        cols = pl.ds(k * PW, PW)
         normed = (res[:, cols].astype(F32) * scale * gained(k)).astype(BF)
         logits = logits + lax.dot_general(
             normed, router_t[:, cols], (((1,), (1,)), ((), ())), preferred_element_type=F32
@@ -213,6 +222,235 @@
         for pr, qr, half in blocks:
             a_wait(pr, qr, half)
 
+    def ds_full(k):
+        return pl.ds(pl.multiple_of(k * CW, CW), CW)
+
+    def ds_half(k, half):
+        return pl.ds(pl.multiple_of(k * CW + half * HW, HW), HW)
+
+    def ds_pack(k):
+        return pl.ds(pl.multiple_of(k * HW, HW), HW)
+
+    def ds_own(k):
+        return pl.ds(pl.multiple_of(k // TURNS * OW, OW), OW)
+
+    def ds_layer(k, layer):
+        return pl.ds(pl.multiple_of(k * CW + layer % OWNERS * OW, OW), OW)
+
+    def q_half(k, side):
+        return remote(
+            t2.at[1:, :, ds_half(k, side)], qh.at[side, 1:, :, ds_pack(k)],
+            b_send.at[0], qh_recv.at[k], on_q(1 - 2 * side),
+        )
+
+    def q_full(k, side):
+        return remote(
+            (t1, t3)[side].at[1:, :, ds_full(k)], qf.at[side, 1:, :, ds_full(k)],
+            b_send.at[1], qf_recv.at[k], on_q(1 - 2 * side),
+        )
+
+    def early_half(k, side):
+        src = t2.at[0, :, pl.ds(pl.multiple_of(k * EW + side * EW // 2, EW // 2), EW // 2)]
+        dst = qh.at[side, 0, :, pl.ds(pl.multiple_of(k * EW // 2, EW // 2), EW // 2)]
+        return remote(src, dst, b_send.at[0], early_recv.at[0, k], on_q(1 - 2 * side))
+
+    def early_full(k, side):
+        cols = pl.ds(pl.multiple_of(k * EW, EW), EW)
+        return remote(
+            (t1, t3)[side].at[0, :, cols], qf.at[side, 0, :, cols],
+            b_send.at[1], early_recv.at[1, k], on_q(1 - 2 * side),
+        )
+
+    def at_end(k):
+        return (k == 0) | (k == LAST)
+
+    def q_direct(k):
+        return remote(
+            t2.at[1:, :, ds_full(k)], qd.at[k // LAST], b_send.at[0], qh_recv.at[k], on_q(2)
+        )
+
+    def p_copy(k, d):
+        return remote(
+            sp.at[d - 1, :, ds_full(k)], pf.at[SIDE - 1 - d, :, ds_full(k)],
+            b_send.at[2], pf_recv.at[k], on_p(d),
+        )
+
+    def owner(k, layer=z):
+        return layer // OWNERS == k % TURNS
+
+    def e_copy(k, layer):
+        return remote(
+            eo.at[:, ds_layer(k, layer)], ec.at[(z + LAYERS - layer) % LAYERS, :, ds_own(k)],
+            b_send.at[3], e_recv.at[k], {"attn": attn, "exp": layer, "mb": c},
+        )
+
+    def o_copy(k, d):
+        mine = om.at[:, ds_layer(k, z)]
+        return remote(mine, mine, b_send.at[4], o_recv.at[int(d not in (2, 6)), k], on_z(d))
+
+    def arrived(ref, sem):
+        remote(ref, ref, b_send.at[0], sem, sibling).wait_recv()
+
+    def left(ref, n):
+        remote(ref, ref, b_send.at[n], out_sem.at[0], sibling).wait_send()
+
+    def down(part, cols):
+        return dot(hid[part, 0:F], wd[0, :, cols]) + dot(hid[part, F:], wd[1, :, cols])
+
+    def down_early(k, carry):
+        cols = pl.ds(pl.multiple_of(k * EW, EW), EW)
+        value = down(slice(0, EARLY), cols).reshape(SIDE, CAP, EW)
+        t2[0, :, cols] = value[AT[0, 2]].astype(BF)
+        early_half(k, 0).start()
+        early_half(k, 1).start()
+        p0[0, :, cols] = value[AT[0, 0]]
+        p1[0, :, cols] = value[AT[0, 1]]
+        p3[0, :, cols] = value[AT[0, 3]]
+        return carry
+
+    def add_early(k, carry):
+        low = pl.ds(pl.multiple_of(k * EW, EW // 2), EW // 2)
+        high = pl.ds(pl.multiple_of(k * EW + EW // 2, EW // 2), EW // 2)
+        pack = pl.ds(pl.multiple_of(k * EW // 2, EW // 2), EW // 2)
+        arrived(qh.at[:, 0, :, pack], early_recv.at[0, k])
+        t1[0, :, low] = (p1[0, :, low] + qh[0, 0, :, pack].astype(F32)).astype(BF)
+        t1[0, :, high] = p1[0, :, high].astype(BF)
+        early_full(k, 0).start()
+        t3[0, :, low] = p3[0, :, low].astype(BF)
+        t3[0, :, high] = (p3[0, :, high] + qh[1, 0, :, pack].astype(F32)).astype(BF)
+        early_full(k, 1).start()
+        return carry
+
+    def stage_down(k):
+        cols = ds_full(k)
+        value = down(slice(EARLY, None), cols).reshape(SIDE * (SIDE - 1), CAP, CW)
+
+        def keep(ref, qr, kind):
+            for n in range(1, SIDE):
+                ref[n, :, cols] = value[AT[STEPS[n], qr] - SIDE].astype(kind)
+
+        keep(t2, 2, BF)
+
+        @pl.when(at_end(k))
+        def _():
+            q_direct(k).start()
+
+        @pl.when(jnp.logical_not(at_end(k)))
+        def _():
+            q_half(k, 0).start()
+            q_half(k, 1).start()
+
+        keep(p1, 1, F32)
+        keep(p3, 3, F32)
+
+        @pl.when(at_end(k))
+        def _():
+            t1[1:, :, cols] = p1[1:, :, cols].astype(BF)
+            q_full(k, 0).start()
+            t3[1:, :, cols] = p3[1:, :, cols].astype(BF)
+            q_full(k, 1).start()
+
+        keep(p0, 0, F32)
+
+    def stage_q_half(k):
+        low, high, pack = ds_half(k, 0), ds_half(k, 1), ds_pack(k)
+
+        @pl.when(jnp.logical_not(at_end(k)))
+        def _():
+            arrived(qh.at[:, 1:, :, pack], qh_recv.at[k])
+            t1[1:, :, low] = (p1[1:, :, low] + qh[0, 1:, :, pack].astype(F32)).astype(BF)
+            t1[1:, :, high] = p1[1:, :, high].astype(BF)
+            q_full(k, 0).start()
+            t3[1:, :, low] = p3[1:, :, low].astype(BF)
+            t3[1:, :, high] = (p3[1:, :, high] + qh[1, 1:, :, pack].astype(F32)).astype(BF)
+            q_full(k, 1).start()
+
+    def stage_q_full(k):
+        cols = ds_full(k)
+        @pl.when(k % SPAN == 0)
+        def _():
+            wide = pl.ds(pl.multiple_of(k // SPAN * EW, EW), EW)
+            arrived(qf.at[:, 0, :, wide], early_recv.at[1, k // SPAN])
+
+        arrived(qf.at[:, 1:, :, cols], qf_recv.at[k])
+
+        @pl.when(at_end(k))
+        def _():
+            arrived(qd.at[0], qh_recv.at[k])
+            p0[1:, :, cols] = p0[1:, :, cols] + qd[k // LAST].astype(F32)
+
+        def summed(n):
+            return p0[n, :, cols] + qf[0, n, :, cols].astype(F32) + qf[1, n, :, cols].astype(F32)
+
+        for n in (3, 1, 2):
+            d = STEPS[n]
+            sp[d - 1, :, cols] = summed(n).astype(BF)
+            p_copy(k, d).start()
+        v0[:, cols] = summed(0)
+
+    def stage_p(k):
+        cols = ds_full(k)
+        arrived(pf.at[:, :, cols], pf_recv.at[k])
+        total = v0[:, cols]
+        for n in range(SIDE - 1):
+            total = total + pf[n, :, cols].astype(F32)
+        eo[:, cols] = total.astype(BF)
+        for n in range(OWNERS):
+            layer = k % TURNS * OWNERS + (z + OWNERS // 2 + n) % OWNERS
+
+            @pl.when(layer != z)
+            def _(layer=layer):
+                e_copy(k, layer).start()
+
+    def stage_mix(k):
+        @pl.when(owner(k))
+        def _():
+            mine = ds_layer(k, z)
+            ec[0, :, ds_own(k)] = eo[:, mine]
+            arrived(ec.at[1:LAYERS, :, ds_own(k)], e_recv.at[k])
+            every = ec[:, :, ds_own(k)].astype(F32).reshape(LAYERS * CAP, OW).astype(BF)
+            both = dot(table[...], every)
+            om[:, mine] = (res[:, mine].astype(F32) + (both[:ROWS] + both[ROWS:])).astype(BF)
+            for d in (2, 6, 1, 7):
+                o_copy(k, d).start()
+
+            @pl.when(k >= RELAYED)
+            def _():
+                for d in (4, 3, 5):
+                    o_copy(k, d).start()
+
+    def out_copy(k):
+        return pltpu.make_async_copy(om.at[:, ds_full(k)], out_h.at[:, ds_full(k)], out_sem.at[0])
+
+    def o_arrived(k, layers, later):
+        ref = om.at[:, pl.ds(pl.multiple_of(k * CW, CW), layers * OW)]
+        arrived(ref, o_recv.at[later, k])
+
+    def stage_relay(k):
+        o_arrived(k, 2 // TURNS, 0)
+        for sign in (1, -1):
+            layer = (z + LAYERS - 2 * sign) % LAYERS
+
+            @pl.when((k < RELAYED) & owner(k, layer))
+            def _(sign=sign, layer=layer):
+                part = om.at[:, ds_layer(k, layer)]
+                half = part.at[pl.ds(ROWS // 4 * (1 - sign), ROWS // 2)]
+                sem = o_recv.at[1, k]
+                remote(part, part, b_send.at[4], sem, on_z(LAYERS + sign)).start()
+                remote(half, half, b_send.at[4], sem, on_z(LAYERS + 2 * sign)).start()
+
+    def stage_out(k):
+        @pl.when(owner(k))
+        def _():
+            o_arrived(k, OWNERS - 1 - 2 // TURNS, 1)
+
+        if TURNS > 1:
+            @pl.when(jnp.logical_not(owner(k)))
+            def _():
+                o_arrived(k, OWNERS - 2 // TURNS, 1)
+
+        out_copy(k).start()
+
     a_wait(1, 0, 0)
     a_copy(1, 0, 0, 2, 0, on_p(-1))
     a_wait(3, 0, 1)
@@ -230,174 +468,32 @@
     spread_q(2, 1)
     loads[4].wait()
     loads[5].wait()
-    a_rest((0, 1, 1), (0, 3, 0))
+    a_rest((0, 1, 1), (0, 3, 0), (0, 2, 0), (0, 2, 1))
     hidden(0, 0)
     forward_q(1)
     siblings[0].wait_recv()
     siblings[1].wait_recv()
     hidden(0, 1)
     forward_q(3)
-    a_rest((0, 2, 0), (0, 2, 1), (1, 1, 1), (1, 3, 0), (3, 1, 1))
+    a_rest((1, 1, 1), (1, 3, 0), (3, 1, 1))
     hidden(1, 0)
     forward_q(2)
+    loads[6].wait()
+    siblings[2].wait_recv()
+    lax.fori_loop(0, D // EW, down_early, 0)
     hidden(1, 1)
     a_rest((3, 3, 0), (2, 1, 1), (2, 3, 0))
     for pr in (1, 3, 2):
         a_rest((pr, 2, 0), (pr, 2, 1))
+    lax.fori_loop(0, D // EW, add_early, 0)
     hidden(2, 0)
     hidden(2, 1)
-    loads[6].wait()
-    siblings[2].wait_recv()
     for copy in siblings:
         copy.wait_send()
     for along_q, ref in enumerate((rows.at[0:3], rows.at[0:12])):
         remote(ref, ref, a_send.at[along_q], a_recv.at[0, 0], sibling).wait_send()
 
-    def ds_full(k):
-        return pl.ds(pl.multiple_of(k * CW, CW), CW)
-
-    def ds_half(k, half):
-        return pl.ds(pl.multiple_of(k * CW + half * HW, HW), HW)
-
-    def ds_pack(k):
-        return pl.ds(pl.multiple_of(k * HW, HW), HW)
-
-    def ds_own(k):
-        return pl.ds(pl.multiple_of(k * OW, OW), OW)
-
-    def ds_layer(k, layer):
-        return pl.ds(pl.multiple_of(k * CW + layer * OW, OW), OW)
-
-    def q_half(k, side):
-        return remote(
-            t2.at[:, :, ds_half(k, side)], qh.at[side, :, :, ds_pack(k)],
-            b_send.at[0], qh_recv.at[k], on_q(1 - 2 * side),
-        )
-
-    def q_full(k, side):
-        return remote(
-            (t1, t3)[side].at[:, :, ds_full(k)], qf.at[side, :, :, ds_full(k)],
-            b_send.at[1], qf_recv.at[k], on_q(1 - 2 * side),
-        )
-
-    def at_end(k):
-        return (k == 0) | (k == LAST)
-
-    def q_direct(k):
-        return remote(
-            t2.at[:, :, ds_full(k)], qd.at[k // LAST], b_send.at[0], qh_recv.at[k], on_q(2)
-        )
-
-    def p_copy(k, d):
-        return remote(
-            sp.at[d - 1, :, ds_full(k)], pf.at[SIDE - 1 - d, :, ds_full(k)],
-            b_send.at[2], pf_recv.at[k], on_p(d),
-        )
-
-    def e_copy(k, d):
-        return remote(
-            eo.at[:, ds_layer(k, (z + d) % LAYERS)], ec.at[LAYERS - d, :, ds_own(k)],
-            b_send.at[3], e_recv.at[k], on_z(d),
-        )
-
-    def o_copy(k, d):
-        mine = om.at[:, ds_layer(k, z)]
-        return remote(mine, mine, b_send.at[4], o_recv.at[k], on_z(d))
-
-    def arrived(ref, sem):
-        remote(ref, ref, b_send.at[0], sem, sibling).wait_recv()
-
-    def left(ref, n):
-        remote(ref, ref, b_send.at[n], out_sem.at[0], sibling).wait_send()
-
-    def stage_down(k):
-        cols = ds_full(k)
-        value = dot(hid[:, 0:F], wd[0, :, cols]) + dot(hid[:, F:], wd[1, :, cols])
-        value = value.reshape(SIDE * SIDE, CAP, CW)
-        for pr in range(SIDE):
-            t2[pr, :, cols] = value[AT[pr, 2]].astype(BF)
-
-        @pl.when(at_end(k))
-        def _():
-            q_direct(k).start()
-
-        @pl.when(jnp.logical_not(at_end(k)))
-        def _():
-            q_half(k, 0).start()
-            q_half(k, 1).start()
-
-        for pr in range(SIDE):
-            p1[pr, :, cols] = value[AT[pr, 1]]
-            p3[pr, :, cols] = value[AT[pr, 3]]
-
-        @pl.when(at_end(k))
-        def _():
-            t1[:, :, cols] = p1[:, :, cols].astype(BF)
-            q_full(k, 0).start()
-            t3[:, :, cols] = p3[:, :, cols].astype(BF)
-            q_full(k, 1).start()
-
-        for pr in range(SIDE):
-            p0[pr, :, cols] = value[AT[pr, 0]]
-
-    def stage_q_half(k):
-        low, high, pack = ds_half(k, 0), ds_half(k, 1), ds_pack(k)
-
-        @pl.when(jnp.logical_not(at_end(k)))
-        def _():
-            arrived(qh.at[:, :, :, pack], qh_recv.at[k])
-            t1[:, :, low] = (p1[:, :, low] + qh[0, :, :, pack].astype(F32)).astype(BF)
-            t1[:, :, high] = p1[:, :, high].astype(BF)
-            q_full(k, 0).start()
-            t3[:, :, low] = p3[:, :, low].astype(BF)
-            t3[:, :, high] = (p3[:, :, high] + qh[1, :, :, pack].astype(F32)).astype(BF)
-            q_full(k, 1).start()
-
-    def stage_q_full(k):
-        cols = ds_full(k)
-        arrived(qf.at[:, :, :, cols], qf_recv.at[k])
-
-        @pl.when(at_end(k))
-        def _():
-            arrived(qd.at[0], qh_recv.at[k])
-            p0[:, :, cols] = p0[:, :, cols] + qd[k // LAST].astype(F32)
-
-        def summed(pr):
-            return p0[pr, :, cols] + qf[0, pr, :, cols].astype(F32) + qf[1, pr, :, cols].astype(F32)
-
-        for d in (2, 1, 3):
-            sp[d - 1, :, cols] = summed(d).astype(BF)
-            p_copy(k, d).start()
-        v0[:, cols] = summed(0)
-
-    def stage_p(k):
-        cols = ds_full(k)
-        arrived(pf.at[:, :, cols], pf_recv.at[k])
-        total = v0[:, cols]
-        for n in range(SIDE - 1):
-            total = total + pf[n, :, cols].astype(F32)
-        eo[:, cols] = total.astype(BF)
-        for d in FAR_FIRST:
-            e_copy(k, d).start()
-
-    def stage_mix(k):
-        mine = ds_layer(k, z)
-        ec[0, :, ds_own(k)] = eo[:, mine]
-        arrived(ec.at[1:LAYERS, :, ds_own(k)], e_recv.at[k])
-        every = ec[:, :, ds_own(k)].astype(F32).reshape(LAYERS * CAP, OW).astype(BF)
-        both = dot(table[...], every)
-        om[:, mine] = (res[:, mine].astype(F32) + (both[:ROWS] + both[ROWS:])).astype(BF)
-        for d in FAR_FIRST:
-            o_copy(k, d).start()
-
-    def out_copy(k):
-        return pltpu.make_async_copy(om.at[:, ds_full(k)], out_h.at[:, ds_full(k)], out_sem.at[0])
-
-    def stage_out(k):
-        arrived(om.at[:, pl.ds(pl.multiple_of(k * CW, CW), (LAYERS - 1) * OW)], o_recv.at[k])
-        out_copy(k).start()
-
-    stages = [stage_down, stage_q_half, stage_q_full, stage_p, stage_mix, stage_out]
+    stages = [stage_down, stage_q_half, stage_q_full, stage_p, stage_mix, stage_relay, stage_out]
 
     def step(i, carry):
         for s, stage in enumerate(stages):
@@ -423,7 +519,7 @@
     left(qf, 1)
     left(pf, 2)
     left(ec.at[1:LAYERS], 3)
-    left(om.at[:, 0 : (LAYERS - 1) * OW * CHUNKS], 4)
+    left(om.at[:, 0 : D // LAYERS * (LAYERS - 1)], 4)
     pltpu.make_async_copy(om, out_h, out_sem.at[0]).wait()
 
 
@@ -455,7 +551,7 @@
             pltpu.VMEM(block, BF),
             pltpu.VMEM((2, SIDE, CAP, HALF), BF),
             pltpu.VMEM((2, SIDE, CAP, D), BF),
-            pltpu.VMEM((2, SIDE, CAP, CW), BF),
+            pltpu.VMEM((2, SIDE - 1, CAP, CW), BF),
             pltpu.VMEM((CAP, D), F32),
             pltpu.VMEM((SIDE - 1, CAP, D), BF),
             pltpu.VMEM((SIDE - 1, CAP, D), BF),
@@ -470,7 +566,8 @@
             dma((SIDE * SIDE, 2)),
             dma((5,)),
         ]
-        + [dma((CHUNKS,))] * 5
+        + [dma((CHUNKS,))] * 4
+        + [dma((2, CHUNKS)), dma((2, D // EW))]
         + [dma((1,))],
         compiler_params=pltpu.CompilerParams(
             collective_id=0, has_side_effects=True, vmem_limit_bytes=60 * 1024 * 1024

time: 87.1 us -> 85 us (0.976)
  Pallas kernels: 84.2 us -> 82.8 us
    pallas_call x1, Pallas kernels: 84.2 us -> 82.8 us  [per_device(): pl.pallas_call(kernel, name='expert_block', out_shape=jax.ShapeDtypeStruc...]
where the time goes in v4:
time: 85 us; the launch traced here: 84.8 us
  Pallas kernels  82.8 us (97%)
  local copies, waits for them, and re-layouts  2.06 us (2%)
    pallas_call x1, Pallas kernels, per_device(): pl.pallas_call(kernel, name='expert_block', out_shape=jax.ShapeDtypeStruc...  82.8 us
    unnamed x1, local copies, waits for them, and re-layouts  2.06 us

profile of v4, /device:TPU:2, one launch (start us, length us, event | category | flops | bytes accessed | tf_op | source)
XLA Modules:
  0.0 84.8 jit_solution(4449006582368533988)
XLA Ops:
  0.0 82.8 %expert_block.1 = bf16[64,6144]{1,0:T(8,128)(2,1)} custom-call(bf16[64,6144]{1,0:T(8,128)(2,1)} %resid_h.1, bf16[6144]{0:T(1024)(128)(2,1)} %gain_h.1, bf16[8,6144]{1,0:T(8,128)(2,1)} %bitcast.2, s32[2,64]{1,0:T(2,128)} %bitcast.3, bf16[1,6144,256]{2,1,0:T(8,128)(2,1)} %wg_h.1, bf16[1,6144,256]{2,1,0:T(8,128)(2,1)} %wu_h.1, bf16[1,256,6144]{2,1,0:T(8,128)(2,1)} %wd_h.1), custom_call_target="tpu_custom_call" | custom-call | tf_op jit(solution)/shard_map/expert_block/pallas_call | solution.py:530
  82.8 2.1 %copy.9 = bf16[64,6144]{1,0:T(8,128)(2,1)} copy(bf16[64,6144]{1,0:T(8,128)(2,1)} %expert_block.1) | data formatting | bytes 1572864

commit v5 on v4

--- a/solution.py
+++ b/solution.py
@@ -410,7 +410,7 @@
             arrived(ec.at[1:LAYERS, :, ds_own(k)], e_recv.at[k])
             every = ec[:, :, ds_own(k)].astype(F32).reshape(LAYERS * CAP, OW).astype(BF)
             both = dot(table[...], every)
-            om[:, mine] = (res[:, mine].astype(F32) + (both[:ROWS] + both[ROWS:])).astype(BF)
+            om[:, mine] = (both[:ROWS] + both[ROWS:]).astype(BF)
             for d in (2, 6, 1, 7):
                 o_copy(k, d).start()
 
@@ -527,7 +527,7 @@
     hbm = pl.BlockSpec(memory_space=pl.ANY)
     dma = pltpu.SemaphoreType.DMA
     block = (SIDE, CAP, D)
-    return pl.pallas_call(
+    total = pl.pallas_call(
         kernel,
         name="expert_block",
         out_shape=jax.ShapeDtypeStruct((ROWS, D), BF),
@@ -575,6 +575,7 @@
     )(
         resid, norm_gain, router.T, expert_ids.T, w_gate, w_up, w_down
     )
+    return (resid.astype(F32) + total.astype(F32)).astype(BF)
 
 
 def solution(mesh):

time: 85 us -> 85 us (level)
  other arithmetic: 0 us -> 2.19 us
  local copies, waits for them, and re-layouts: 2.06 us -> 0.01 us
    convert_element_type x0 -> x1, other arithmetic: none -> 2.19 us  [per_device(): return (resid.astype(F32) + total.astype(F32)).astype(BF)]
    unnamed x1 -> x2, local copies, waits for them, and re-layouts: 2.06 us -> 0.01 us
where the time goes in v5:
time: 85 us; the launch traced here: 84.9 us
  Pallas kernels  82.7 us (97%)
  other arithmetic  2.19 us (3%)
    pallas_call x1, Pallas kernels, per_device(): pl.pallas_call(kernel, name='expert_block', out_shape=jax.ShapeDtypeStruc...  82.7 us
    convert_element_type x1, other arithmetic, per_device(): return (resid.astype(F32) + total.astype(F32)).astype(BF)  2.19 us

profile of v5, /device:TPU:2, one launch (start us, length us, event | category | flops | bytes accessed | tf_op | source)
XLA Modules:
  0.0 84.9 jit_solution(9496818079684597590)
XLA Ops:
  0.0 0.0 copy-start
  0.0 82.7 %expert_block.1 = bf16[64,6144]{1,0:T(8,128)(2,1)} custom-call(bf16[64,6144]{1,0:T(8,128)(2,1)} %resid_h.1, bf16[6144]{0:T(1024)(128)(2,1)} %gain_h.1, bf16[8,6144]{1,0:T(8,128)(2,1)} %bitcast.2, s32[2,64]{1,0:T(2,128)} %bitcast.3, bf16[1,6144,256]{2,1,0:T(8,128)(2,1)} %wg_h.1, bf16[1,6144,256]{2,1,0:T(8,128)(2,1)} %wu_h.1, bf16[1,256,6144]{2,1,0:T(8,128)(2,1)} %wd_h.1), custom_call_target="tpu_custom_call" | custom-call | tf_op jit(solution)/shard_map/expert_block/pallas_call | solution.py:530
  82.7 0.0 copy-done
  82.7 2.2 %add_convert_fusion = bf16[64,6144]{1,0:T(8,128)(2,1)} fusion(bf16[64,6144]{1,0:T(8,128)(2,1)} %expert_block.1, bf16[64,6144]{1,0:T(8,128)(2,1)S(1)} %copy-done), kind=kLoop, calls=%fused_computation | loop fusion | flops 1572864 | bytes 2359296 | tf_op jit(solution)/shard_map/convert_element_type | solution.py:578
Async XLA Ops:
  0.0 82.7 %copy-start = (bf16[64,6144]{1,0:T(8,128)(2,1)S(1)}, bf16[64,6144]{1,0:T(8,128)(2,1)}, u32[]{:S(2)}) copy-start(bf16[64,6144]{1,0:T(8,128)(2,1)} %resid_h.1) | copy-start | bytes 2359300
